TPU v7x, 128 devices: a whole 4x4x4 slice. The times are simulated.
128 devices in a mesh: tm: 4 (over x_hi, core), height: 32 (over y, x_lo, z).
Axes of the slice: x: 4 (x_hi: 2, x_lo: 2; x = x_hi * 2 + x_lo), y: 4, z: 4, core: 2. Of those that a mesh axis runs over, the one named last changes fastest.
Arguments:
- tokens: bfloat16 [32, 448, 14, 256], P('tm', 'height'), may hold values from -6 to 6
- region_ids: int32 [32, 448, 14], P('tm', 'height'), may hold values from 0 to 26, as said below
- first_gain: float32 [256], replicated, may hold values from 0.5 to 1.5
- first_bias: float32 [256], replicated, may hold values from -1.5 to 1.5
- input_weight: bfloat16 [256, 768], replicated, may hold values from -0.375 to 0.375
- input_bias: float32 [768], replicated, may hold values from -1.5 to 1.5
- output_weight: bfloat16 [256, 256], replicated, may hold values from -0.375 to 0.375
- output_bias: float32 [256], replicated, may hold values from -1.5 to 1.5
- second_gain: float32 [256], replicated, may hold values from 0.5 to 1.5
- second_bias: float32 [256], replicated, may hold values from -1.5 to 1.5
- expand_weight: bfloat16 [256, 1024], replicated, may hold values from -0.375 to 0.375
- expand_bias: float32 [1024], replicated, may hold values from -1.5 to 1.5
- reduce_weight: bfloat16 [1024, 256], replicated, may hold values from -0.1875 to 0.1875
- reduce_bias: float32 [256], replicated, may hold values from -1.5 to 1.5
- merge_gain: float32 [1024], replicated, may hold values from 0.5 to 1.5
- merge_bias: float32 [1024], replicated, may hold values from -1.5 to 1.5
- merge_weight: bfloat16 [1024, 512], replicated, may hold values from -0.1875 to 0.1875
- cotangent: bfloat16 [32, 224, 7, 512], P(None, 'height', None, 'tm'), may hold values from -6 to 6
Outputs:
- merged: bfloat16 [32, 224, 7, 512], P(None, 'height', None, 'tm')
- grad_tokens: bfloat16 [32, 448, 14, 256], P('tm', 'height')
- grad_first_gain: float32 [256], replicated
- grad_first_bias: float32 [256], replicated
- grad_input_weight: float32 [256, 768], replicated
- grad_input_bias: float32 [768], replicated
- grad_output_weight: float32 [256, 256], replicated
- grad_output_bias: float32 [256], replicated
- grad_second_gain: float32 [256], replicated
- grad_second_bias: float32 [256], replicated
- grad_expand_weight: float32 [256, 1024], replicated
- grad_expand_bias: float32 [1024], replicated
- grad_reduce_weight: float32 [1024, 256], replicated
- grad_reduce_bias: float32 [256], replicated
- grad_merge_gain: float32 [1024], replicated
- grad_merge_bias: float32 [1024], replicated
- grad_merge_weight: float32 [1024, 512], replicated
Inputs may be any that keep to these rules, and one draw needn't show every extreme that they name: `region_ids`: swin shift-region labels of the shifted grid: 9 a + 3 b + c, where a, b, c in 0 to 2 tell in which slab a cell's frame, row and column lies ([0, n - w), [n - w, n - w / 2), [n - w / 2, n) for a dimension of n cells and windows of w cells); about one cell in eight holds an arbitrary label instead.
All inputs are finite; a program needn't handle non-finite values.
Results may differ from a plain program's by a relative error of at most 0.024.
Values may be sent and summed in bfloat16 or wider, within the bound.
No kernel may reach another device: no remote copies, remote signals or barrier semaphores. Data moves between devices by JAX's collectives and lax.ppermute only.
A program may use at most 128 MiB of HBM per device.

v0:
```python
import math

import jax
import jax.numpy as jnp
from jax import lax
from jax.sharding import PartitionSpec as P

HEADS = 8
WIN_H = 7
WIN_W = 7


NORM_EPS = 1e-05


def from_behind(value, axis, steps):
    count = lax.axis_size(axis)
    pairs = [(source, (source + steps) % count) for source in range(count)]
    return lax.ppermute(value, axis, pairs)


def layer_norm(inputs, norm_gain, norm_bias):
    widened = inputs.astype(jnp.float32)
    average = jnp.mean(widened, -1, keepdims=True)
    centred = widened - average
    variance = jnp.mean(centred * centred, -1, keepdims=True)
    return (centred * lax.rsqrt(variance + NORM_EPS) * norm_gain + norm_bias).astype(jnp.bfloat16)


def window_core(queries, keys_in, values_in, labels):
    factor = queries.shape[-1] ** (-0.5)
    scores = (
        jnp.einsum("gqhd,gkhd->ghqk", queries, keys_in, preferred_element_type=jnp.float32) * factor
    )
    allowed = (labels[:, :, None] == labels[:, None, :])[:, None]
    weights = jnp.where(allowed, jnp.exp(scores), 0.0)
    probs = (weights / jnp.sum(weights, -1, keepdims=True)).astype(jnp.bfloat16)
    return jnp.einsum(
        "ghqk,gkhd->gqhd", probs, values_in, preferred_element_type=jnp.float32
    ).astype(jnp.bfloat16)


def attend_block(shifted, region_block, input_weight, input_bias, output_weight, output_bias):
    frames, row_total, col_total, channels = shifted.shape
    row_wins = row_total // WIN_H
    col_wins = col_total // WIN_W
    count = row_wins * col_wins
    window_size = frames * WIN_H * WIN_W
    head_width = channels // HEADS
    windows = shifted.reshape(frames, row_wins, WIN_H, col_wins, WIN_W, channels)
    windows = windows.transpose(1, 3, 0, 2, 4, 5).reshape(count * window_size, channels)
    labels = region_block.reshape(frames, row_wins, WIN_H, col_wins, WIN_W)
    labels = labels.transpose(1, 3, 0, 2, 4).reshape(count // 2, 2, window_size)
    packed = (
        jnp.dot(windows, input_weight, preferred_element_type=jnp.float32) + input_bias
    ).astype(jnp.bfloat16)
    packed = packed.reshape(count // 2, 2, window_size, 3, HEADS, head_width)
    checked = jax.checkpoint(window_core)
    context = lax.map(
        lambda grouped: checked(grouped[0], grouped[1], grouped[2], grouped[3]),
        (packed[:, :, :, 0], packed[:, :, :, 1], packed[:, :, :, 2], labels),
    )
    context = context.reshape(count * window_size, channels)
    output = (
        jnp.dot(context, output_weight, preferred_element_type=jnp.float32) + output_bias
    ).astype(jnp.bfloat16)
    output = output.reshape(row_wins, col_wins, frames, WIN_H, WIN_W, channels)
    return output.transpose(2, 0, 3, 1, 4, 5).reshape(frames, row_total, col_total, channels)


def post_block(
    block_tokens,
    restored,
    second_gain,
    second_bias,
    expand_weight,
    expand_bias,
    reduce_weight,
    reduce_bias,
    merge_gain,
    merge_bias,
    merge_weight,
):
    frames, row_total, col_total, channels = block_tokens.shape
    residual = (block_tokens.astype(jnp.float32) + restored.astype(jnp.float32)).astype(
        jnp.bfloat16
    )
    residual = residual.reshape(-1, channels)
    second_normed = layer_norm(residual, second_gain, second_bias)
    hidden = jax.nn.gelu(
        jnp.dot(second_normed, expand_weight, preferred_element_type=jnp.float32) + expand_bias,
        approximate=False,
    ).astype(jnp.bfloat16)
    block_out = (
        residual.astype(jnp.float32)
        + jnp.dot(hidden, reduce_weight, preferred_element_type=jnp.float32)
        + reduce_bias
    ).astype(jnp.bfloat16)
    quadrants = block_out.reshape(frames, row_total // 2, 2, col_total // 2, 2, channels)
    gathered = jnp.concatenate(
        [
            quadrants[:, :, 0, :, 0],
            quadrants[:, :, 1, :, 0],
            quadrants[:, :, 0, :, 1],
            quadrants[:, :, 1, :, 1],
        ],
        -1,
    )
    merge_normed = layer_norm(gathered, merge_gain, merge_bias)
    merged = jnp.dot(
        merge_normed.reshape(-1, 4 * channels), merge_weight, preferred_element_type=jnp.float32
    ).astype(jnp.bfloat16)
    return merged.reshape(frames, row_total // 2, col_total // 2, 2 * channels)


def widen(grad_part):
    return grad_part.astype(jnp.float32)


def local(
    tokens,
    region_ids,
    first_gain,
    first_bias,
    input_weight,
    input_bias,
    output_weight,
    output_bias,
    second_gain,
    second_bias,
    expand_weight,
    expand_bias,
    reduce_weight,
    reduce_bias,
    merge_gain,
    merge_bias,
    merge_weight,
    cotangent,
):
    frames = tokens.shape[0]
    row_total = tokens.shape[1]
    lead_t = frames // 2
    lead_h = WIN_H // 2
    lead_w = WIN_W // 2

    def move_ahead(field):
        ahead_part = from_behind(field[:lead_t], "tm", -1)
        field = jnp.concatenate([field[lead_t:], ahead_part], 0)
        above_part = from_behind(field[:, :lead_h], "height", -1)
        field = jnp.concatenate([field[:, lead_h:], above_part], 1)
        return jnp.roll(field, -lead_w, 2)

    def move_back(field):
        behind_part = from_behind(field[frames - lead_t :], "tm", 1)
        field = jnp.concatenate([behind_part, field[: frames - lead_t]], 0)
        below_part = from_behind(field[:, row_total - lead_h :], "height", 1)
        field = jnp.concatenate([below_part, field[:, : row_total - lead_h]], 1)
        return jnp.roll(field, lead_w, 2)

    def attend_local(shifted_in, weight_in, bias_in, weight_out, bias_out):
        return attend_block(shifted_in, region_ids, weight_in, bias_in, weight_out, bias_out)

    normed, norm_back = jax.vjp(layer_norm, tokens, first_gain, first_bias)
    shifted = move_ahead(normed)
    attended, attend_back = jax.vjp(
        attend_local, shifted, input_weight, input_bias, output_weight, output_bias
    )
    restored = move_back(attended)
    local_merged, post_back = jax.vjp(
        post_block,
        tokens,
        restored,
        second_gain,
        second_bias,
        expand_weight,
        expand_bias,
        reduce_weight,
        reduce_bias,
        merge_gain,
        merge_bias,
        merge_weight,
    )
    merged = lax.all_to_all(local_merged, "tm", split_axis=3, concat_axis=0, tiled=True)
    local_cot = lax.all_to_all(cotangent, "tm", split_axis=0, concat_axis=3, tiled=True)
    (
        cot_tokens,
        cot_restored,
        grad_second_gain,
        grad_second_bias,
        grad_expand_weight,
        grad_expand_bias,
        grad_reduce_weight,
        grad_reduce_bias,
        grad_merge_gain,
        grad_merge_bias,
        grad_merge_weight,
    ) = post_back(local_cot)
    merged_count = (
        cotangent.shape[0] * cotangent.shape[1] * cotangent.shape[2] * lax.axis_size("height")
    )
    factor = 1.0 / math.sqrt(merged_count)
    cot_attended = move_ahead(cot_restored)
    cot_shifted, grad_input_weight, grad_input_bias, grad_output_weight, grad_output_bias = (
        attend_back(cot_attended)
    )
    cot_normed = move_back(cot_shifted)
    cot_from_norm, grad_first_gain, grad_first_bias = norm_back(cot_normed)
    grad_tokens = cot_tokens + cot_from_norm
    totals = lax.psum(
        (
            widen(grad_first_gain),
            widen(grad_first_bias),
            widen(grad_input_weight),
            widen(grad_input_bias),
            widen(grad_output_weight),
            widen(grad_output_bias),
            widen(grad_second_gain),
            widen(grad_second_bias),
            widen(grad_expand_weight),
            widen(grad_expand_bias),
            widen(grad_reduce_weight),
            widen(grad_reduce_bias),
            widen(grad_merge_gain),
            widen(grad_merge_bias),
            widen(grad_merge_weight),
        ),
        ("tm", "height"),
    )
    scaled = [total_part * factor for total_part in totals]
    return (
        merged,
        grad_tokens,
        scaled[0],
        scaled[1],
        scaled[2],
        scaled[3],
        scaled[4],
        scaled[5],
        scaled[6],
        scaled[7],
        scaled[8],
        scaled[9],
        scaled[10],
        scaled[11],
        scaled[12],
        scaled[13],
        scaled[14],
    )


def solution(mesh):
    in_specs = (
        P("tm", "height", None, None),
        P("tm", "height", None),
        P(),
        P(),
        P(),
        P(),
        P(),
        P(),
        P(),
        P(),
        P(),
        P(),
        P(),
        P(),
        P(),
        P(),
        P(),
        P(None, "height", None, "tm"),
    )
    out_specs = (
        P(None, "height", None, "tm"),
        P("tm", "height", None, None),
        P(),
        P(),
        P(),
        P(),
        P(),
        P(),
        P(),
        P(),
        P(),
        P(),
        P(),
        P(),
        P(),
        P(),
        P(),
    )
    return jax.shard_map(local, mesh=mesh, in_specs=in_specs, out_specs=out_specs, check_vma=False)
```

profile of v0, /device:TPU:1, one launch (start us, length us, event | category | flops | bytes accessed | tf_op | source)
XLA Modules:
  0.0 492.4 jit_solution(16970879759416995664)
XLA Ops:
  12.4 8.3 %collective-permute-done = bf16[4,14,14,256]{3,0,2,1:T(4,128)(2,1)S(1)} collective-permute-done((bf16[4,14,14,256]{3,0,2,1:T(4,128)(2,1)S(1)}, bf16[4,14,14,256]{3,0,2,1:T(4,128)(2,1)S(1)}, u32[]{:S(2)}, u32[]{:S(2)}) %collective-permute-start) | collective-permute-done | bytes 401440 | tf_op jit(solution)/shard_map/ppermute | solution.py:19
  20.7 7.1 %collective-permute-start.1 = (bf16[8,3,14,256]{3,0,2,1:T(8,128)(2,1)S(1)}, bf16[8,3,14,256]{3,0,2,1:T(8,128)(2,1)S(1)}, u32[]{:S(2)}, u32[]{:S(2)}) collective-permute-start(bf16[8,3,14,256]{3,0,2,1:T(8,128)(2,1)S(1)} %pad_maximum_fusion.14), channel_id=1, source_target_pairs={{0,31},{1,0},{2,1},{3,2},{4,3},{5,4},{6,5},{7,6},{8,7},{9,8},{10,9... | collective-permute-start | bytes 516104 | tf_op jit(solution)/shard_map/ppermute | solution.py:19
  36.2 4.7 copy.190
  40.9 11.1 %reshape.318 = bf16[2,2,392,3,8,32]{2,1,0,5,4,3:T(2,128)(2,1)} reshape(bf16[1568,768]{0,1:T(8,128)(2,1)} %copy.190) | data formatting | bytes 4816896 | tf_op jit(solution)/shard_map/jvp()/reshape | solution.py:57
  58.7 20.1 %while.29 = (s32[]{:T(128)}, bf16[2,2,392,8,32]{2,1,0,4,3:T(2,128)(2,1)}, bf16[2,2,392,8,32]{2,4,3,1,0:T(8,128)(2,1)}, s32[2,2,392]{2,1,0:T(2,128)S(1)}, bf16[2,...) while((s32[]{:T(128)}, bf16[2,2,392,8,32]{2,1,0,4,3:T(2,128)(2,1)}, ...), condition=%wide.region_4.5_spmd, body=%wide.region_2.4_spmd.sunk | while | flops 332416000 | bytes 36514804 | solution.py:59
  59.0 4.8 fusion.152
  69.0 4.8 fusion.152
  96.4 7.6 %all-to-all-done.1 = bf16[32,7,7,128]{3,2,1,0:T(8,128)(2,1)S(1)} async-done(((bf16[32,7,7,128]{3,2,1,0:T(8,128)(2,1)}), bf16[32,7,7,128]{3,2,1,0:T(8,128)(2,1)S(1)}, u32[]{:S(2)}, u32[]{:S(2)}) %all-to-all-start.1) | async-done | bytes 401440 | tf_op jit(solution)/shard_map/all_to_all | solution.py:184
  105.3 6.4 %collective-permute-done.3 = bf16[8,3,14,256]{3,0,2,1:T(8,128)(2,1)} collective-permute-done((bf16[8,3,14,256]{3,0,2,1:T(8,128)(2,1)S(1)}, bf16[8,3,14,256]{3,0,2,1:T(8,128)(2,1)}, u32[]{:S(2)}, u32[]{:S(2)}) %collective-permute-start.3) | collective-permute-done | bytes 172064 | tf_op jit(solution)/shard_map/ppermute | solution.py:19
  118.7 16.9 %multiply_convert_fusion = (bf16[1568,1024]{1,0:T(8,128)(2,1)S(1)}, f32[1568,1024]{1,0:T(8,128)}, f32[1568,1024]{1,0:T(8,128)}) fusion(f32[1024]{0:T(1024)S(1)} %copy-done.96, bf16[256,1024]{1,0:T(8,128)(2,1)S(1)} %copy-done.91, f32[1568,256]{1,0:T(8,128)S(1)} %reshape.333, f32[256]{0:T(256)S(1)} %copy-done.102, f32[256]{0:T(256)S(1)} %copy-done.87, ...), kind=kOutput, calls=%fused_computation.65 | convolution fusion | flops 930062336 | bytes 18204928 | tf_op jit(solution)/shard_map/jvp()/dot_general | solution.py:91
  138.6 4.7 slice_reduce_fusion.3
  159.5 7.3 %fusion.102 = (f32[1024]{0:T(1024)}, bf16[1568,1024]{1,0:T(8,128)(2,1)S(1)}) fusion(f32[1568,1024]{1,0:T(8,128)} %get-tuple-element.416, bf16[1568,256]{1,0:T(8,128)(2,1)S(1)} %reshape.326, bf16[1024,256]{1,0:T(8,128)(2,1)S(1)} %copy-done.90, f32[1568,1024]{1,0:T(8,128)} %get-tuple-element.453, f32[1024]{0:T(1024)S(1)} %copy-done.97), kind=kOutput, calls=%fused_computation.239 | convolution fusion | flops 850983936 | bytes 17391616 | tf_op jit(solution)/shard_map/transpose(jvp())/dot_general | solution.py:96
  179.6 5.4 %collective-permute-done.4 = bf16[4,14,14,256]{3,2,1,0:T(8,128)(2,1)S(1)} collective-permute-done((bf16[4,14,14,256]{3,2,1,0:T(8,128)(2,1)}, bf16[4,14,14,256]{3,2,1,0:T(8,128)(2,1)S(1)}, u32[]{:S(2)}, u32[]{:S(2)}) %collective-permute-start.4) | collective-permute-done | bytes 401440 | tf_op jit(solution)/shard_map/ppermute | solution.py:19
  186.2 6.9 %copy.211 = bf16[8,7,7,512]{2,0,1,3:T(8,128)(2,1)} copy(bf16[8,7,7,512]{3,2,1,0:T(8,128)(2,1)S(1)} %reshape.324) | data formatting | bytes 802816 | tf_op jit(solution)/shard_map/jvp()/reshape | solution.py:113
  193.1 12.3 %reshape.340 = bf16[4,2,25088]{2,1,0:T(2,128)(2,1)} reshape(bf16[512,7,8,7]{3,2,1,0:T(8,128)(2,1)} %bitcast.194) | data formatting | bytes 802816
  219.1 48.0 %while.30 = (s32[]{:T(128)}, bf16[2,2,392,8,32]{2,4,3,1,0:T(8,128)(2,1)}, bf16[2,2,392,8,32]{2,4,3,1,0:T(8,128)(2,1)}, bf16[2,2,392,8,32]{2,4,3,1,0:T(8,128)(2,1...) while((s32[]{:T(128)}, ...), condition=%wide.region_16.17_spmd, body=%wide.region_13.16_spmd.sunk | while | flops 841363712 | bytes 98249216 | solution.py:59
  229.1 4.6 fusion.163
  233.7 4.5 fusion.164
  253.1 4.6 fusion.163
  257.7 4.5 fusion.164
  287.3 19.3 %reshape.341 = bf16[512,7,8,7]{3,2,1,0:T(8,128)(2,1)} reshape(bf16[4,2,25088]{2,1,0:T(2,128)(2,1)} %all-to-all-done) | data formatting | bytes 802816
  306.6 8.9 %copy.212 = bf16[8,7,7,512]{3,0,2,1:T(8,128)(2,1)} copy(bf16[8,7,7,512]{2,0,1,3:T(8,128)(2,1)} %bitcast.193) | data formatting | bytes 802816 | tf_op jit(solution)/shard_map/all_to_all | solution.py:183
  332.8 63.0 %all-reduce.7 = (f32[256]{0:T(256)S(1)}, f32[256]{0:T(256)S(1)}, f32[768]{0:T(1024)S(1)}, f32[256]{0:T(256)S(1)}, f32[256]{0:T(256)S(1)}, /*index=5*/f32[256]{0:...) all-reduce(f32[256]{0:T(256)S(1)} %get-tuple-element.350, ...), channel_id=1, replica_groups=mesh['tm'=4,'height'=32] {'tm','height'}, use_global_device_ids=true, to_apply=%region_20.21 | all-reduce | flops 5376 | bytes 43008 | tf_op jit(solution)/shard_map/psum | solution.py:209
  403.4 75.3 %all-reduce.11.cloned.1.call-done = (f32[256,768]{1,0:T(8,128)}, f32[256,256]{1,0:T(8,128)}, f32[256,1024]{1,0:T(8,128)}, f32[1024,256]{1,0:T(8,128)}, f32[1024,512]{1,0:T(8,128)}) async-done(((f32[256,768]{1,0:T(8,128)}, f32[256,256]{1,0:T(8,128)}, f32[256,1024]{1,0:T(8,128)}, f32[1024,256]{1,0:T(8,128)}, f32[1024,512]{1,0:T(8,128)}), (f32[256,768]{1,0:T(8,128)}, f32[256,256]{1,0:T(8,128)}, ...) | async-done | bytes 5242896 | tf_op jit(solution)/shard_map/psum | solution.py:209
  (409 shorter events, 183.5 us)
Async XLA Ops:
  7.2 138.5 %copy-start = (bf16[1024,512]{1,0:T(8,128)(2,1)S(1)}, bf16[1024,512]{1,0:T(8,128)(2,1)}, u32[]{:S(2)}) copy-start(bf16[1024,512]{1,0:T(8,128)(2,1)} %param.38) | copy-start | bytes 3145732
  10.6 17.3 %copy-start.59 = (s32[8,14,14]{2,0,1:T(8,128)S(1)}, s32[8,14,14]{2,0,1:T(8,128)}, u32[]{:S(2)}) copy-start(s32[8,14,14]{2,0,1:T(8,128)} %param.23) | copy-start | bytes 18820
  10.9 9.8 %collective-permute-start = (bf16[4,14,14,256]{3,0,2,1:T(4,128)(2,1)S(1)}, bf16[4,14,14,256]{3,0,2,1:T(4,128)(2,1)S(1)}, u32[]{:S(2)}, u32[]{:S(2)}) collective-permute-start(bf16[4,14,14,256]{3,0,2,1:T(4,128)(2,1)S(1)} %get-tuple-element.447), channel_id=1, source_target_pairs={{0,96},{32,0},{64,32},{96,64},{1,97},{33,1},{65,33},{97,65},{2,98}... | collective-permute-start | bytes 1204232 | tf_op jit(solution)/shard_map/ppermute | solution.py:19
  20.7 10.6 %collective-permute-start.1 = (bf16[8,3,14,256]{3,0,2,1:T(8,128)(2,1)S(1)}, bf16[8,3,14,256]{3,0,2,1:T(8,128)(2,1)S(1)}, u32[]{:S(2)}, u32[]{:S(2)}) collective-permute-start(bf16[8,3,14,256]{3,0,2,1:T(8,128)(2,1)S(1)} %pad_maximum_fusion.14), channel_id=1, source_target_pairs={{0,31},{1,0},{2,1},{3,2},{4,3},{5,4},{6,5},{7,6},{8,7},{9,8},{10,9... | collective-permute-start | bytes 516104 | tf_op jit(solution)/shard_map/ppermute | solution.py:19
  89.7 5.8 %collective-permute-start.2 = (bf16[4,14,14,256]{3,0,2,1:T(4,128)(2,1)}, bf16[4,14,14,256]{3,0,2,1:T(4,128)(2,1)S(1)}, u32[]{:S(2)}, u32[]{:S(2)}) collective-permute-start(bf16[4,14,14,256]{3,0,2,1:T(4,128)(2,1)} %bitcast.25), channel_id=1, source_target_pairs={{0,32},{32,64},{64,96},{96,0},{1,33},{33,65},{65,97},{97,1},{2,34}... | collective-permute-start | bytes 1204232 | tf_op jit(solution)/shard_map/ppermute | solution.py:19
  91.1 12.9 %all-to-all-start.1 = ((bf16[32,7,7,128]{3,2,1,0:T(8,128)(2,1)}), bf16[32,7,7,128]{3,2,1,0:T(8,128)(2,1)S(1)}, u32[]{:S(2)}, u32[]{:S(2)}) async-start(bf16[32,7,7,128]{3,2,1,0:T(8,128)(2,1)} %copy.213), calls=%async_computation.1 | async-start | bytes 917504 | tf_op jit(solution)/shard_map/all_to_all | solution.py:184
  96.3 15.3 %collective-permute-start.3 = (bf16[8,3,14,256]{3,0,2,1:T(8,128)(2,1)S(1)}, bf16[8,3,14,256]{3,0,2,1:T(8,128)(2,1)}, u32[]{:S(2)}, u32[]{:S(2)}) collective-permute-start(bf16[8,3,14,256]{3,0,2,1:T(8,128)(2,1)S(1)} %pad_maximum_fusion.13), channel_id=1, source_target_pairs={{0,1},{1,2},{2,3},{3,4},{4,5},{5,6},{6,7},{7,8},{8,9},{9,10},{10,1... | collective-permute-start | bytes 516104 | tf_op jit(solution)/shard_map/ppermute | solution.py:19
  118.7 16.9 %copy-start.14 = (f32[1568,256]{1,0:T(8,128)}, f32[1568,256]{1,0:T(8,128)S(1)}, u32[]{:S(2)}) copy-start(f32[1568,256]{1,0:T(8,128)S(1)} %reshape.333) | copy-start | bytes 4816900
  118.7 18.6 %copy-start.89 = (bf16[1024,256]{1,0:T(8,128)(2,1)S(1)}, bf16[1024,256]{1,0:T(8,128)(2,1)}, u32[]{:S(2)}) copy-start(bf16[1024,256]{1,0:T(8,128)(2,1)} %param.34) | copy-start | bytes 1572868
  118.7 18.6 %copy-start.101 = (f32[256]{0:T(256)S(1)}, f32[256]{0:T(256)}, u32[]{:S(2)}) copy-start(f32[256]{0:T(256)} %param.35) | copy-start | bytes 3076
  174.7 10.4 %collective-permute-start.4 = (bf16[4,14,14,256]{3,2,1,0:T(8,128)(2,1)}, bf16[4,14,14,256]{3,2,1,0:T(8,128)(2,1)S(1)}, u32[]{:S(2)}, u32[]{:S(2)}) collective-permute-start(bf16[4,14,14,256]{3,2,1,0:T(8,128)(2,1)} %slice.139), channel_id=1, source_target_pairs={{0,96},{32,0},{64,32},{96,64},{1,97},{33,1},{65,33},{97,65},{2,98}... | collective-permute-start | bytes 1204232 | tf_op jit(solution)/shard_map/ppermute | solution.py:19
  175.3 9.9 %copy-start.39 = (bf16[392,256]{1,0:T(8,128)(2,1)S(1)}, bf16[392,256]{1,0:T(8,128)(2,1)}, u32[]{:S(2)}) copy-start(bf16[392,256]{1,0:T(8,128)(2,1)} %copy-done.38) | copy-start | bytes 602116
  175.3 9.9 %copy-start.42 = (bf16[392,256]{1,0:T(8,128)(2,1)S(1)}, bf16[392,256]{1,0:T(8,128)(2,1)}, u32[]{:S(2)}) copy-start(bf16[392,256]{1,0:T(8,128)(2,1)} %copy-done.41) | copy-start | bytes 602116
  175.3 9.9 %copy-start.45 = (bf16[392,256]{1,0:T(8,128)(2,1)S(1)}, bf16[392,256]{1,0:T(8,128)(2,1)}, u32[]{:S(2)}) copy-start(bf16[392,256]{1,0:T(8,128)(2,1)} %copy-done.44) | copy-start | bytes 602116
  175.4 9.9 %copy-start.48 = (bf16[392,256]{1,0:T(8,128)(2,1)S(1)}, bf16[392,256]{1,0:T(8,128)(2,1)}, u32[]{:S(2)}) copy-start(bf16[392,256]{1,0:T(8,128)(2,1)} %copy-done.47) | copy-start | bytes 602116
  175.4 9.9 %copy-start.71 = (f32[1024]{0:T(1024)S(1)}, f32[1024]{0:T(1024)}, u32[]{:S(2)}) copy-start(f32[1024]{0:T(1024)} %param.36) | copy-start | bytes 12292
  175.4 9.9 %copy-start.74 = (f32[392]{0:T(512)S(1)}, f32[392]{0:T(512)}, u32[]{:S(2)}) copy-start(f32[392]{0:T(512)} %copy-done.73) | copy-start | bytes 4708
  175.4 9.9 %copy-start.77 = (f32[392]{0:T(512)S(1)}, f32[392]{0:T(512)}, u32[]{:S(2)}) copy-start(f32[392]{0:T(512)} %copy-done.76) | copy-start | bytes 4708
  185.1 24.6 %collective-permute-start.5 = (bf16[8,3,14,256]{3,2,1,0:T(8,128)(2,1)S(1)}, bf16[8,3,14,256]{3,2,1,0:T(8,128)(2,1)S(1)}, u32[]{:S(2)}, u32[]{:S(2)}) collective-permute-start(bf16[8,3,14,256]{3,2,1,0:T(8,128)(2,1)S(1)} %slice.170), channel_id=1, source_target_pairs={{0,31},{1,0},{2,1},{3,2},{4,3},{5,4},{6,5},{7,6},{8,7},{9,8},{10,9... | collective-permute-start | bytes 516104 | tf_op jit(solution)/shard_map/ppermute | solution.py:19
  205.5 81.8 %all-to-all-start = ((bf16[4,2,25088]{2,1,0:T(2,128)(2,1)}), bf16[4,2,25088]{2,1,0:T(2,128)(2,1)}, u32[]{:S(2)}, u32[]{:S(2)}) async-start(bf16[4,2,25088]{2,1,0:T(2,128)(2,1)} %reshape.340), calls=%async_computation | async-start | bytes 802816 | tf_op jit(solution)/shard_map/all_to_all | solution.py:183
  209.6 269.1 %all-reduce.11.cloned.1.call-start = ((), (), s32[]{:S(2)}) async-start(), calls=%async_computation.2 | async-start | bytes 10485760 | tf_op jit(solution)/shard_map/psum | solution.py:209
  281.5 37.8 %collective-permute-start.6 = (bf16[4,14,14,256]{3,0,2,1:T(4,128)(2,1)}, bf16[4,14,14,256]{3,0,2,1:T(4,128)(2,1)S(1)}, u32[]{:S(2)}, u32[]{:S(2)}) collective-permute-start(bf16[4,14,14,256]{3,0,2,1:T(4,128)(2,1)} %bitcast.46), channel_id=1, source_target_pairs={{0,32},{32,64},{64,96},{96,0},{1,33},{33,65},{65,97},{97,1},{2,34}... | collective-permute-start | bytes 1204232 | tf_op jit(solution)/shard_map/ppermute | solution.py:19
  320.1 8.8 %collective-permute-start.7 = (bf16[8,3,14,256]{3,0,2,1:T(8,128)(2,1)}, bf16[8,3,14,256]{3,0,2,1:T(8,128)(2,1)}, u32[]{:S(2)}, u32[]{:S(2)}) collective-permute-start(bf16[8,3,14,256]{3,0,2,1:T(8,128)(2,1)} %pad_maximum_fusion.12), channel_id=1, source_target_pairs={{0,1},{1,2},{2,3},{3,4},{4,5},{5,6},{6,7},{7,8},{8,9},{9,10},{10,1... | collective-permute-start | bytes 516104 | tf_op jit(solution)/shard_map/ppermute | solution.py:19
  331.4 70.1 %copy-start.67 = (f32[256]{0:T(256)S(1)}, f32[256]{0:T(256)}, u32[]{:S(2)}) copy-start(f32[256]{0:T(256)} %param.24) | copy-start | bytes 3076
  (101 other events, 319.8 us)
Sparse Core Ops, SparseCore 0:
  323.4 155.2 all-reduce.10
where the time goes:
time: 502 us; the launch traced here: 492 us
  local copies, waits for them, and re-layouts  134 us (27%)
  waiting for transfers between devices  110 us (22%)
  matrix products  99.3 us (20%)
  blocking collectives  63 us (13%)
  other arithmetic  47.9 us (10%)
  starting transfers between devices  22.8 us (5%)
  between operations  15.7 us (3%)
    psum x1, waiting for transfers between devices, local(): lax.psum((widen(grad_first_gain), widen(grad_first_bias), widen(grad_inpu...  75.3 us
    psum x1, blocking collectives, local(): lax.psum((widen(grad_first_gain), widen(grad_first_bias), widen(grad_inpu...  63 us
    unnamed x198, local copies, waits for them, and re-layouts  40.6 us
    ppermute x8, waiting for transfers between devices, from_behind(): return lax.ppermute(value, axis, pairs)  26.6 us
    dot_general x8, matrix products, window_core(): jnp.einsum('gqhd,gkhd->ghqk', queries, keys_in, preferred_element_type=jn...  24.5 us
    dot_general x6, matrix products, window_core(): jnp.einsum('ghqk,gkhd->gqhd', probs, values_in, preferred_element_type=jn...  22.1 us
    dot_general x3, matrix products, post_block(): jnp.dot(second_normed, expand_weight, preferred_element_type=jnp.float32)  21.5 us
    reshape x2, local copies, waits for them, and re-layouts, attend_block(): packed = packed.reshape(count // 2, 2, window_size, 3, HEADS, head_width)  15.1 us
  transfers between devices with their start and end apart: 11, of which 7 were waited for; matrix products, arithmetic and copies ran while one was open for 29% of the time, Pallas kernels for 0%

commit v1 on v0

v1 whole, which is shorter than its diff:
```python
import functools
import math

import jax
import jax.numpy as jnp
from jax import lax
from jax.experimental import pallas as pl
from jax.experimental.pallas import tpu as pltpu
from jax.sharding import PartitionSpec as P

F32 = jnp.float32
BF16 = jnp.bfloat16
NORM_EPS = 1e-05
DIM = 256
CELLS = 392
TILES = 49
FAR = 2.0**100
SCORE_SCALE = math.log2(math.e) / math.sqrt(32.0)
MIB = 1 << 20


def dot(a, b):
    return lax.dot_general(a, b, (((1,), (0,)), ((), ())), preferred_element_type=F32)


def dot_nt(a, b):
    return lax.dot_general(a, b, (((1,), (1,)), ((), ())), preferred_element_type=F32)


def dot_tn(a, b):
    return lax.dot_general(a, b, (((0,), (0,)), ((), ())), preferred_element_type=F32)


def row(ref):
    return ref[...].reshape(1, -1)


def norm_stats(x):
    average = jnp.mean(x, -1, keepdims=True)
    centred = x - average
    rstd = lax.rsqrt(jnp.mean(centred * centred, -1, keepdims=True) + NORM_EPS)
    return centred * rstd, rstd


def norm_back(dxhat, xhat, rstd):
    first = jnp.mean(dxhat, -1, keepdims=True)
    second = jnp.mean(dxhat * xhat, -1, keepdims=True)
    return (dxhat - first - xhat * second) * rstd


def lanes(rows):
    return lax.broadcasted_iota(jnp.int32, (rows, 128), 1)


def head_mask(index):
    return (lanes(1) // 32 == index).astype(BF16)


def three_parts(value, lane, start):
    high = value.astype(BF16).astype(F32)
    middle = (value - high).astype(BF16).astype(F32)
    low = value - high - middle
    return jnp.where(lane < start + 8, high, jnp.where(lane < start + 16, middle, low))


def attend_kernel(
    tok_ref, lab_ref, gain_ref, bias_ref, wi_ref, bi_ref, wo_ref, bo_ref,
    res_ref, x_ref, qkv_ref, ctx_ref, eq_ref, field,
):
    for f in range(8):
        for r in range(7):
            start = (f * 7 + r) * 16
            cells = tok_ref[f, r].astype(F32)
            for half in range(2):
                field[half, start : start + 14, :] = cells[:, 128 * half : 128 * half + 128]

    def window(win, carry):
        parts = []
        for wi in range(7):
            for wj in range(7):
                column = lax.rem(win * 7 + wj + 3, 14)
                parts.append(
                    jnp.concatenate(
                        [field[s, pl.ds(wi * 16 + column, 8, stride=112), :] for s in range(2)],
                        1,
                    )
                )
        x = jnp.concatenate(parts, 0)
        x_ref[win] = x.astype(BF16)
        xhat, _ = norm_stats(x)
        normed = (xhat * row(gain_ref) + row(bias_ref)).astype(BF16)
        packed = dot(normed, wi_ref[...]) + row(bi_ref)
        q = (packed[:, 0:256] * SCORE_SCALE).astype(BF16)
        k = packed[:, 256:512].astype(BF16)
        v = packed[:, 512:768]
        vb = v.astype(BF16)
        vs = (v * (2.0**-12)).astype(BF16)
        qkv_ref[win, :, 0:256] = q
        qkv_ref[win, :, 256:512] = k
        qkv_ref[win, :, 512:768] = vb
        label = lab_ref[win]
        lane = lanes(CELLS)
        same = lane == label
        eq32 = jnp.where(same | (lane == 27), 1.0, 0.0)
        eq = eq32.astype(BF16)
        ek = jnp.where(
            lane < 27, jnp.where(same, 0.0, -FAR), jnp.where(lane == 27, -1.0, 0.0)
        ).astype(BF16)
        ones = jnp.ones((CELLS, 128), BF16)
        sums = jnp.ones((CELLS, 128), F32)
        halves = []
        for t in range(2):
            qt = q[:, 128 * t : 128 * t + 128]
            kaug = jnp.concatenate([k[:, 128 * t : 128 * t + 128], ek], 1)
            vaug = jnp.concatenate([vs[:, 128 * t : 128 * t + 128], ones], 1)
            half = jnp.zeros((CELLS, 128), F32)
            for hh in range(4):
                h = 4 * t + hh
                qaug = jnp.concatenate([qt * head_mask(hh), eq], 1)
                p = jnp.exp2(dot_nt(qaug, kaug)).astype(BF16)
                pv = dot(p, vaug)
                total = pv[:, 128:256]
                half = jnp.where(lane // 32 == hh, pv[:, 0:128] * (4096.0 / total), half)
                sums = jnp.where((lane >= 32) & (lane < 56) & (lane % 8 == h), total, sums)
            halves.append(half)
        ctx = jnp.concatenate(halves, 1).astype(BF16)
        ctx_ref[win] = ctx
        minus = three_parts(-jnp.log2(sums), lane, 32)
        eq_ref[win] = jnp.where((lane >= 32) & (lane < 56), minus, eq32).astype(BF16)
        attended = (dot(ctx, wo_ref[...]) + row(bo_ref)).astype(BF16)
        res_ref[win] = (x + attended.astype(F32)).astype(BF16)
        return carry

    lax.fori_loop(0, 2, window, 0)


def whole(shape):
    return pl.BlockSpec(shape, lambda i, n=len(shape): (0,) * n)


def attend(row_win, field, labels, gain, bias, wi, bi, wo, bo):
    outs = [(2, CELLS, 256), (2, CELLS, 256), (2, CELLS, 768), (2, CELLS, 256), (2, CELLS, 128)]
    return pl.pallas_call(
        attend_kernel,
        grid=(1,),
        in_specs=[
            pl.BlockSpec((8, 7, 14, 256), lambda i: (0, row_win, 0, 0)),
            pl.BlockSpec((2, CELLS, 1), lambda i: (row_win, 0, 0)),
            whole((256,)),
            whole((256,)),
            whole((256, 768)),
            whole((768,)),
            whole((256, 256)),
            whole((256,)),
        ],
        out_specs=[whole(s) for s in outs],
        out_shape=[jax.ShapeDtypeStruct(s, BF16) for s in outs],
        scratch_shapes=[pltpu.VMEM((2, 896, 128), F32)],
        compiler_params=pltpu.CompilerParams(vmem_limit_bytes=48 * MIB),
        cost_estimate=pl.CostEstimate(flops=8 * 10**9, bytes_accessed=8 * 10**6, transcendentals=2500000),
    )(field, labels, gain, bias, wi, bi, wo, bo)


def attend_back_kernel(
    d_ref, x_ref, qkv_ref, ctx_ref, eq_ref, lab_ref, gain_ref, bias_ref, wi_ref, wo_ref,
    out_ref, dwi_ref, dwo_ref, vec_ref, field, dwi, dwo, vec,
):
    dwi[...] = jnp.zeros_like(dwi)
    dwo[...] = jnp.zeros_like(dwo)
    vec[...] = jnp.zeros_like(vec)

    def window(win, carry):
        d = d_ref[win]
        d32 = d.astype(F32)
        ctx = ctx_ref[win]
        dwo[...] += dot_tn(ctx, d)
        vec[3:4, 0:256] += jnp.sum(d32, 0, keepdims=True)
        dctx = dot_nt(d, wo_ref[...]).astype(BF16)
        product = dctx.astype(F32) * ctx.astype(F32)
        high = product.astype(BF16)
        low = (product - high.astype(F32)).astype(BF16)
        picks_r = lax.broadcasted_iota(jnp.int32, (256, 128), 0) // 32
        picks_c = lax.broadcasted_iota(jnp.int32, (256, 128), 1)
        picks = ((picks_c < 24) & (picks_c % 8 == picks_r)).astype(BF16)
        lane = lanes(CELLS)
        delta = three_parts(-(dot(high, picks) + dot(low, picks)), lane, 0)
        dd = jnp.where(lane < 24, delta, 0.0).astype(BF16)
        eq = eq_ref[win]
        same = lane == lab_ref[win]
        ek = jnp.where(lane < 27, jnp.where(same, 0.0, -FAR), jnp.where(lane == 27, -1.0, 0.0))
        lane1 = lanes(1)
        dqs, dks, dvs = [], [], []
        for t in range(2):
            cols = slice(128 * t, 128 * t + 128)
            qt = qkv_ref[win, :, 128 * t : 128 * t + 128]
            kt = qkv_ref[win, :, 256 + 128 * t : 256 + 128 * t + 128]
            vt = qkv_ref[win, :, 512 + 128 * t : 512 + 128 * t + 128]
            dot_t = dctx[:, cols]
            qaug = jnp.concatenate([qt, eq], 1)
            daug = jnp.concatenate([dot_t, dd], 1)
            ktt = jnp.transpose(kt.astype(F32)).astype(BF16)
            dk = jnp.zeros((CELLS, 128), F32)
            dv = jnp.zeros((CELLS, 128), F32)
            dqt = []
            for hh in range(4):
                h = 4 * t + hh
                mask = head_mask(hh)
                picked = (lane1 >= 32) & (lane1 < 56) & (lane1 % 8 == h)
                kaug = jnp.concatenate([kt * mask, jnp.where(picked, 1.0, ek).astype(BF16)], 1)
                tail = jnp.where((lane < 24) & (lane % 8 == h), 1.0, 0.0).astype(BF16)
                vaug = jnp.concatenate([vt * mask, tail], 1)
                p = jnp.exp2(dot_nt(kaug, qaug))
                ds = (p * dot_nt(vaug, daug)).astype(BF16)
                dv = dv + dot(p.astype(BF16), dot_t * mask)
                dk = dk + dot(ds, qt * mask)
                dqt.append(dot(ktt[32 * hh : 32 * hh + 32, :], ds))
            dqs.append(jnp.transpose(jnp.concatenate(dqt, 0)))
            dks.append(dk)
            dvs.append(dv)
        dpacked32 = jnp.concatenate(
            [d_q * (1.0 / math.sqrt(32.0)) for d_q in dqs]
            + [d_k * math.log(2.0) for d_k in dks]
            + dvs,
            1,
        )
        dpacked = dpacked32.astype(BF16)
        vec[2:3, :] += jnp.sum(dpacked32, 0, keepdims=True)
        x = x_ref[win].astype(F32)
        xhat, rstd = norm_stats(x)
        gain = row(gain_ref)
        normed = (xhat * gain + row(bias_ref)).astype(BF16)
        dwi[...] += dot_tn(normed, dpacked)
        dnormed = dot_nt(dpacked, wi_ref[...]).astype(BF16).astype(F32)
        vec[0:1, 0:256] += jnp.sum(dnormed * xhat, 0, keepdims=True)
        vec[1:2, 0:256] += jnp.sum(dnormed, 0, keepdims=True)
        dx = norm_back(dnormed * gain, xhat, rstd).astype(BF16).astype(F32) + d32
        for wi in range(7):
            for wj in range(7):
                column = lax.rem(win * 7 + wj + 3, 14)
                at = (wi * 7 + wj) * 8
                for s in range(2):
                    field[s, pl.ds(wi * 16 + column, 8, stride=112), :] = dx[at : at + 8, 128 * s : 128 * s + 128]
        return carry

    lax.fori_loop(0, 2, window, 0)
    for f in range(8):
        for r in range(7):
            start = (f * 7 + r) * 16
            halves = [field[s, start : start + 14, :] for s in range(2)]
            out_ref[f, r] = jnp.concatenate(halves, 1).astype(BF16)
    for s in range(6):
        dwi_ref[s] = dwi[:, 128 * s : 128 * s + 128].astype(F32)
    for s in range(2):
        dwo_ref[s] = dwo[:, 128 * s : 128 * s + 128].astype(F32)
    vec_ref[...] = vec[...]


def attend_back(row_win, d, x, qkv, ctx, eq, labels, gain, bias, wi, wo):
    outs = [
        ((8, 7, 14, 256), BF16),
        ((6, 256, 128), F32),
        ((2, 256, 128), F32),
        ((8, 768), F32),
    ]
    return pl.pallas_call(
        attend_back_kernel,
        grid=(1,),
        in_specs=[
            whole((2, CELLS, 256)),
            whole((2, CELLS, 256)),
            whole((2, CELLS, 768)),
            whole((2, CELLS, 256)),
            whole((2, CELLS, 128)),
            pl.BlockSpec((2, CELLS, 1), lambda i: (row_win, 0, 0)),
            whole((256,)),
            whole((256,)),
            whole((256, 768)),
            whole((256, 256)),
        ],
        out_specs=[whole(s) for s, _ in outs],
        out_shape=[jax.ShapeDtypeStruct(s, t) for s, t in outs],
        scratch_shapes=[
            pltpu.VMEM((2, 896, 128), F32),
            pltpu.VMEM((256, 768), F32),
            pltpu.VMEM((256, 256), F32),
            pltpu.VMEM((8, 768), F32),
        ],
        compiler_params=pltpu.CompilerParams(vmem_limit_bytes=48 * MIB),
        cost_estimate=pl.CostEstimate(flops=20 * 10**9, bytes_accessed=8 * 10**6, transcendentals=2500000),
    )(d, x, qkv, ctx, eq, labels, gain, bias, wi, wo)


def gelu_pair(v):
    half_square = jnp.exp2(v * v * (-0.5 * math.log2(math.e)))
    t = 1.0 / (1.0 + jnp.abs(v) * (0.3275911 * math.sqrt(0.5)))
    poly = t * (0.5 * 0.254829592 + t * (0.5 * -0.284496736 + t * (0.5 * 1.421413741 + t * (0.5 * -1.453152027 + t * (0.5 * 1.061405429)))))
    tail = poly * half_square
    phi = jnp.where(v >= 0.0, 1.0 - tail, tail)
    return v * phi, phi + v * half_square * (1.0 / math.sqrt(2.0 * math.pi))


QUADRANTS = ((0, 0), (1, 0), (0, 1), (1, 1))


def tile_start(r, c):
    s = (c - 3) % 14
    return ((s // 7) * 14 + r) * 56 + (s % 7) * 8


def post_kernel(
    above_ref, res0_ref, res1_ref, cot_ref, sg_ref, sb_ref, we_ref, be_ref, wr_ref, br_ref, mg_ref, mb_ref, wm_ref,
    merged_ref, dabove_ref, d0_ref, d1_ref, dwe_ref, dwr_ref, dwm_ref, vec_ref,
    field, sn_all, hid_all, dbo_all, dpre_all, mn_all, dm_all, vec,
):
    for wc in range(2):
        base = wc * 784
        field[base : base + 168, :] = above_ref[wc].astype(F32)
        field[base + 168 : base + 560, :] = res0_ref[wc].astype(F32)
        field[base + 560 : base + 784, :] = res1_ref[wc, 0:224, :].astype(F32)
    vec[...] = jnp.zeros_like(vec)
    sg, sb, be, br = row(sg_ref), row(sb_ref), row(be_ref), row(br_ref)

    def chunk(i, carry):
        starts = []
        for rp, cp in QUADRANTS:
            for j in range(7):
                starts.append(pl.multiple_of(tile_start(0, 2 * j + cp) + (2 * i + rp) * 56, 8))
        x = jnp.concatenate([field[pl.ds(s, 8), :] for s in starts], 0)
        xhat, rstd = norm_stats(x)
        sn = (xhat * sg + sb).astype(BF16)
        here = pl.multiple_of(i * 224, 16)
        sn_all[pl.ds(here, 224), :] = sn
        hidden, slope = gelu_pair(dot(sn, we_ref[...]) + be)
        hidden = hidden.astype(BF16)
        hid_all[pl.ds(here, 224), :] = hidden
        out = (x + dot(hidden, wr_ref[...]) + br).astype(BF16).astype(F32)
        gathered = jnp.concatenate([out[56 * q : 56 * q + 56, :] for q in range(4)], 1)
        mhat, mrstd = norm_stats(gathered)
        mg = row(mg_ref)
        mn = mhat * mg + row(mb_ref)
        merged = dot(mn.astype(BF16), wm_ref[...])
        pad = pl.multiple_of(i * 64, 64)
        mn_all[pl.ds(pad, 64), :] = jnp.concatenate([mn, jnp.zeros((8, 1024), F32)], 0).astype(BF16)
        for s in range(4):
            merged_ref[s, i] = merged[:, 128 * s : 128 * s + 128].astype(BF16)
        dm32 = jnp.concatenate([cot_ref[s, i].astype(F32) for s in range(4)], 1)
        dm_all[pl.ds(pad, 64), :] = jnp.concatenate([dm32, jnp.zeros((8, 512), F32)], 0).astype(BF16)
        dmn = dot_nt(dm32.astype(BF16), wm_ref[...]).astype(BF16).astype(F32)
        vec[4:5, :] += jnp.sum(dmn * mhat, 0, keepdims=True)
        vec[5:6, :] += jnp.sum(dmn, 0, keepdims=True)
        dgathered = norm_back(dmn * mg, mhat, mrstd)
        dbo32 = jnp.concatenate([dgathered[:, 256 * q : 256 * q + 256] for q in range(4)], 0)
        dbo = dbo32.astype(BF16)
        dbo32 = dbo.astype(F32)
        dbo_all[pl.ds(here, 224), :] = dbo
        vec[3:4, 0:256] += jnp.sum(dbo32, 0, keepdims=True)
        dpre32 = dot_nt(dbo, wr_ref[...]) * slope
        vec[2:3, :] += jnp.sum(dpre32, 0, keepdims=True)
        dpre = dpre32.astype(BF16)
        dpre_all[pl.ds(here, 224), :] = dpre
        dsn = dot_nt(dpre, we_ref[...]).astype(BF16).astype(F32)
        vec[0:1, 0:256] += jnp.sum(dsn * xhat, 0, keepdims=True)
        vec[1:2, 0:256] += jnp.sum(dsn, 0, keepdims=True)
        dx = dbo32 + norm_back(dsn * sg, xhat, rstd)
        for n, s in enumerate(starts):
            field[pl.ds(s, 8), :] = dx[8 * n : 8 * n + 8, :]
        return carry

    lax.fori_loop(0, 7, chunk, 0)
    for wc in range(2):
        base = wc * 784
        dabove_ref[wc] = field[base : base + 168, :].astype(BF16)
        d0_ref[wc] = field[base + 168 : base + 560, :].astype(BF16)
        d1_ref[wc] = field[base + 560 : base + 784, :].astype(BF16)
    for s in range(8):
        dwe_ref[s] = dot_tn(sn_all[...], dpre_all[:, 128 * s : 128 * s + 128]).astype(BF16)
    dwr = dot_tn(hid_all[...], dbo_all[...])
    for s in range(2):
        dwr_ref[s] = dwr[:, 128 * s : 128 * s + 128].astype(BF16)
    dwm = dot_tn(mn_all[...], dm_all[...])
    for s in range(4):
        dwm_ref[s] = dwm[:, 128 * s : 128 * s + 128].astype(BF16)
    vec_ref[...] = vec[...]


def post(above, res0, res1, cot, *params):
    outs = [
        ((4, 7, 56, 128), BF16),
        ((2, 168, 256), BF16),
        ((2, CELLS, 256), BF16),
        ((2, 224, 256), BF16),
        ((8, 256, 128), BF16),
        ((2, 1024, 128), BF16),
        ((4, 1024, 128), BF16),
        ((8, 1024), F32),
    ]
    ins = (above, res0, res1, cot) + params
    return pl.pallas_call(
        post_kernel,
        grid=(1,),
        in_specs=[whole(a.shape) for a in ins],
        out_specs=[whole(s) for s, _ in outs],
        out_shape=[jax.ShapeDtypeStruct(s, t) for s, t in outs],
        scratch_shapes=[
            pltpu.VMEM((1568, 256), F32),
            pltpu.VMEM((1568, 256), BF16),
            pltpu.VMEM((1568, 1024), BF16),
            pltpu.VMEM((1568, 256), BF16),
            pltpu.VMEM((1568, 1024), BF16),
            pltpu.VMEM((448, 1024), BF16),
            pltpu.VMEM((448, 512), BF16),
            pltpu.VMEM((8, 1024), F32),
        ],
        compiler_params=pltpu.CompilerParams(vmem_limit_bytes=56 * MIB),
        cost_estimate=pl.CostEstimate(flops=15 * 10**9, bytes_accessed=20 * 10**6, transcendentals=3200000),
    )(*ins)


def split_frames_kernel(cot_ref, out_ref, field):
    for f in range(36):
        for i in range(7):
            start = (f * 7 + i) * 8
            field[start : start + 7, :] = cot_ref[f % 32, i].astype(F32)
    for d in range(4):
        for i in range(7):
            tiles = [
                field[pl.ds(((8 * d + 4) * 7 + i) * 8 + j, 8, stride=56), :] for j in range(7)
            ]
            out_ref[d, i] = jnp.concatenate(tiles, 0).astype(BF16)


def split_frames(cotangent):
    return pl.pallas_call(
        split_frames_kernel,
        out_shape=jax.ShapeDtypeStruct((4, 7, 56, 128), BF16),
        scratch_shapes=[pltpu.VMEM((2016, 128), F32)],
    )(cotangent)


def join_frames_kernel(parts_ref, out_ref, field):
    for d in range(4):
        for i in range(7):
            tiles = parts_ref[d, i].astype(F32)
            for j in range(7):
                field[pl.ds(((8 * d + 4) * 7 + i) * 8 + j, 8, stride=56), :] = tiles[8 * j : 8 * j + 8]
    for f in range(32):
        source = f + 32 if f < 4 else f
        for i in range(7):
            start = (source * 7 + i) * 8
            out_ref[f, i] = field[start : start + 7, :].astype(BF16)


def join_frames(parts):
    return pl.pallas_call(
        join_frames_kernel,
        out_shape=jax.ShapeDtypeStruct((32, 7, 7, 128), BF16),
        scratch_shapes=[pltpu.VMEM((2016, 128), F32)],
    )(parts)


def moved(value, axis, steps):
    sizes = [lax.axis_size(a) for a in axis]
    total = math.prod(sizes)
    pairs = []
    for source in range(total):
        if len(axis) == 1:
            pairs.append((source, (source + steps) % total))
        else:
            t, h = divmod(source, sizes[1])
            pairs.append((source, ((t + steps) % sizes[0]) * sizes[1] + (h + steps) % sizes[1]))
    return lax.ppermute(value, axis if len(axis) > 1 else axis[0], pairs)


TM = ("tm",)
ROWS = ("height",)
BOTH = ("tm", "height")


def spread_sum(slabs, factor):
    n = slabs.shape[0] // 128
    parts = lax.all_to_all(slabs.reshape(128, n, 128), BOTH, 0, 0, tiled=True)
    total = (jnp.sum(parts.astype(F32), 0) * factor).astype(BF16)
    copies = jnp.broadcast_to(total[None], (128, n, 128))
    return lax.all_to_all(copies, BOTH, 0, 0, tiled=True).reshape(128 * n, 128)


def local(
    tokens, region_ids, first_gain, first_bias, input_weight, input_bias, output_weight, output_bias,
    second_gain, second_bias, expand_weight, expand_bias, reduce_weight, reduce_bias, merge_gain, merge_bias,
    merge_weight, cotangent,
):
    merged_count = cotangent.shape[0] * cotangent.shape[1] * cotangent.shape[2] * lax.axis_size("height")
    factor = 1.0 / math.sqrt(merged_count)

    from_tm = moved(tokens[:4, 3:], TM, -1)
    from_rows = moved(tokens[4:, :3], ROWS, -1)
    from_both = moved(tokens[:4, :3], BOTH, -1)
    field = jnp.concatenate(
        [
            jnp.concatenate([tokens[4:, 3:], from_rows], 1),
            jnp.concatenate([from_tm, from_both], 1),
        ],
        0,
    )
    labels = region_ids.reshape(8, 2, 7, 2, 7).transpose(1, 3, 2, 4, 0).reshape(4, CELLS, 1)
    cot = lax.all_to_all(split_frames(cotangent), "tm", 0, 0, tiled=True)

    attn = (first_gain, first_bias, input_weight, input_bias, output_weight, output_bias)
    res1, x1, qkv1, ctx1, eq1 = attend(1, field, labels, *attn)
    above = moved(res1[:, 224:], ROWS, 1)
    res0, x0, qkv0, ctx0, eq0 = attend(0, field, labels, *attn)
    merged_parts, dabove, d0, d1, dwe, dwr, dwm, vec_post = post(
        above, res0, res1, cot, second_gain, second_bias, expand_weight, expand_bias, reduce_weight,
        reduce_bias, merge_gain, merge_bias, merge_weight,
    )
    below = moved(dabove, ROWS, -1)
    merged = join_frames(lax.all_to_all(merged_parts, "tm", 0, 0, tiled=True))

    back = (first_gain, first_bias, input_weight, output_weight)
    g0, dwi0, dwo0, vec0 = attend_back(0, d0, x0, qkv0, ctx0, eq0, labels, *back)
    g1, dwi1, dwo1, vec1 = attend_back(
        1, jnp.concatenate([d1, below], 1), x1, qkv1, ctx1, eq1, labels, *back
    )

    grad = jnp.concatenate([g0, g1], 1)
    to_tm = moved(grad[4:, :11], TM, 1)
    to_rows = moved(grad[:4, 11:], ROWS, 1)
    to_both = moved(grad[4:, 11:], BOTH, 1)
    grad_tokens = jnp.concatenate(
        [
            jnp.concatenate([to_both, to_tm], 1),
            jnp.concatenate([to_rows, grad[:4, :11]], 1),
        ],
        0,
    )

    vec_attn = vec0 + vec1
    vectors = jnp.concatenate(
        [
            vec_attn[0, :256],
            vec_attn[1, :256],
            vec_attn[2],
            vec_attn[3, :256],
            vec_post[0, :256],
            vec_post[1, :256],
            vec_post[2],
            vec_post[3, :256],
            vec_post[4],
            vec_post[5],
        ]
    ).reshape(42, 128)
    slabs = jnp.concatenate(
        [
            dwe.reshape(2048, 128),
            dwr.reshape(2048, 128),
            dwm.reshape(4096, 128),
            (dwi0 + dwi1).astype(BF16).reshape(1536, 128),
            (dwo0 + dwo1).astype(BF16).reshape(512, 128),
            jnp.pad(vectors, ((0, 1024 - 42), (0, 0))).astype(BF16),
        ],
        0,
    )
    sums = spread_sum(slabs, factor).astype(F32)

    def unslab(start, count, rows):
        part = sums[start : start + count * rows].reshape(count, rows, 128)
        return part.transpose(1, 0, 2).reshape(rows, count * 128)

    flat = sums[10240:10282].reshape(42 * 128)
    ends = [256, 512, 1280, 1536, 1792, 2048, 3072, 3328, 4352]
    vecs = jnp.split(flat, ends)
    return (
        merged,
        grad_tokens,
        vecs[0],
        vecs[1],
        unslab(8192, 6, 256),
        vecs[2],
        unslab(9728, 2, 256),
        vecs[3],
        vecs[4],
        vecs[5],
        unslab(0, 8, 256),
        vecs[6],
        unslab(2048, 2, 1024),
        vecs[7],
        vecs[8],
        vecs[9],
        unslab(4096, 4, 1024),
    )


def solution(mesh):
    in_specs = (
        (P("tm", "height", None, None), P("tm", "height", None))
        + (P(),) * 15
        + (P(None, "height", None, "tm"),)
    )
    out_specs = (P(None, "height", None, "tm"), P("tm", "height", None, None)) + (P(),) * 15
    return jax.shard_map(local, mesh=mesh, in_specs=in_specs, out_specs=out_specs, check_vma=False)
```

time: 502 us -> 235 us (0.47); the launches traced: 492 us -> 234 us
  matrix products: 99.3 us -> 0 us
  local copies, waits for them, and re-layouts: 134 us -> 41.3 us
  waiting for transfers between devices: 110 us -> 40 us
  Pallas kernels: 0 us -> 64.9 us
  other arithmetic: 47.9 us -> 5.49 us
  blocking collectives: 63 us -> 43.7 us
  starting transfers between devices: 22.8 us -> 37.4 us
  between operations: 15.7 us -> 1.18 us
    dot_general x29 -> x0, matrix products: 99.4 us -> none  [the longest x8 24.5 us: window_core(): jnp.einsum('gqhd,gkhd->ghqk', queries, keys_in, preferred_element_type=jn...]
    psum x1 -> x0, waiting for transfers between devices: 75.3 us -> none  [local(): lax.psum((widen(grad_first_gain), widen(grad_first_bias), widen(grad_inpu...]
    pallas_call x0 -> x7, Pallas kernels: none -> 64.9 us  [the longest x1 26.9 us: post(): pl.pallas_call(post_kernel, grid=(1,), in_specs=[whole(a.shape) for a in...]
    psum x1 -> x0, blocking collectives: 63 us -> none  [local(): lax.psum((widen(grad_first_gain), widen(grad_first_bias), widen(grad_inpu...]
    all_to_all x0 -> x1, blocking collectives: none -> 43.7 us  [spread_sum(): parts = lax.all_to_all(slabs.reshape(128, n, 128), BOTH, 0, 0, tiled=True)]
    reshape x15 -> x2, local copies, waits for them, and re-layouts: 32.8 us -> 0.39 us  [local(): region_ids.reshape(8, 2, 7, 2, 7).transpose(1, 3, 2, 4, 0)]
    mul x17 -> x0, other arithmetic: 21.5 us -> none  [the longest x15 12.4 us: local(): scaled = [total_part * factor for total_part in totals]]
    reduce_sum x13 -> x1, other arithmetic: 17.3 us -> 2.27 us  [spread_sum(): total = (jnp.sum(parts.astype(F32), 0) * factor).astype(BF16)]
  transfers between devices with their start and end apart: 11 -> 11, of which waited for: 7 -> 2; matrix products, arithmetic and copies ran while one was open for 29% -> 7% of each run, Pallas kernels for 0% -> 11%
where the time goes in v1:
time: 235 us; the launch traced here: 234 us
  Pallas kernels  64.9 us (28%)
  blocking collectives  43.7 us (19%)
  local copies, waits for them, and re-layouts  41.3 us (18%)
  waiting for transfers between devices  40 us (17%)
  starting transfers between devices  37.4 us (16%)
  other arithmetic  5.49 us (2%)
    all_to_all x1, blocking collectives, spread_sum(): parts = lax.all_to_all(slabs.reshape(128, n, 128), BOTH, 0, 0, tiled=True)  43.7 us
    ppermute x8, waiting for transfers between devices, moved(): return lax.ppermute(value, axis if len(axis) > 1 else axis[0], pairs)  34.1 us
    pallas_call x1, Pallas kernels, post(): pl.pallas_call(post_kernel, grid=(1,), in_specs=[whole(a.shape) for a in...  26.9 us
    unnamed x83, local copies, waits for them, and re-layouts  26.6 us
    pallas_call x2, Pallas kernels, attend_back(): pl.pallas_call(attend_back_kernel, grid=(1,), in_specs=[whole((2, CELLS,...  22.9 us
    ppermute x8, starting transfers between devices, moved(): return lax.ppermute(value, axis if len(axis) > 1 else axis[0], pairs)  22.5 us
    pallas_call x2, Pallas kernels, attend(): pl.pallas_call(attend_kernel, grid=(1,), in_specs=[pl.BlockSpec((8, 7, 14...  11.1 us
    all_to_all x1, waiting for transfers between devices, local(): merged = join_frames(lax.all_to_all(merged_parts, 'tm', 0, 0, tiled=True))  5.89 us
  transfers between devices with their start and end apart: 11, of which 2 were waited for; matrix products, arithmetic and copies ran while one was open for 7% of the time, Pallas kernels for 11%

profile of v1, /device:TPU:1, one launch (start us, length us, event | category | flops | bytes accessed | tf_op | source)
XLA Modules:
  0.0 234.0 jit_solution(5800010966280278685)
XLA Ops:
  4.9 8.7 %collective-permute-start.2 = (bf16[4,3,14,256]{3,2,1,0:T(8,128)(2,1)S(1)}, bf16[4,3,14,256]{3,2,1,0:T(8,128)(2,1)S(1)}, u32[]{:S(2)}, u32[]{:S(2)}) collective-permute-start(bf16[4,3,14,256]{3,2,1,0:T(8,128)(2,1)S(1)} %copy.82), channel_id=1, source_target_pairs={{0,127},{1,96},{2,97},{3,98},{4,99},{5,100},{6,101},{7,102},{8,103... | collective-permute-start | bytes 258056 | tf_op jit(solution)/shard_map/ppermute | solution.py:471
  14.8 2.0 shard_map.307
  16.8 4.9 %all-to-all-start = ((bf16[4,7,56,128]{3,2,1,0:T(8,128)(2,1)}), bf16[4,7,56,128]{3,2,1,0:T(8,128)(2,1)}, u32[]{:S(2)}, u32[]{:S(2)}) async-start(bf16[4,7,56,128]{3,2,1,0:T(8,128)(2,1)} %shard_map.307), calls=%async_computation | async-start | bytes 802816 | tf_op jit(solution)/shard_map/all_to_all | solution.py:506
  22.6 5.6 %shard_map.305 = (bf16[2,392,256]{2,1,0:T(8,128)(2,1)S(1)}, bf16[2,392,256]{2,1,0:T(8,128)(2,1)S(1)}, bf16[2,392,768]{2,1,0:T(8,128)(2,1)S(1)}, bf16[2,392,256]{2,1,0:T(8,128)(2,1)S(1)}, bf16[2,392,128]{2,1,0:T(8,128)(2,1)S(1)}) custom-call(bf16[8,14,14,256]{3,2,1,0:T(8,128)(2,1)S(1)} %maximum_maximum_fusion.tok_ref, s32[4,392,1]{2,1,0:T(8,128)S(1)} %reshape.130.lab_ref, ...), custom_call_target="tpu_custom_call" | custom-call | flops 8000000000 | bytes 8000000 | tf_op jit(solution)/shard_map/pallas_call | solution.py:143
  31.4 5.5 %shard_map.306 = (bf16[2,392,256]{2,1,0:T(8,128)(2,1)S(1)}, bf16[2,392,256]{2,1,0:T(8,128)(2,1)S(1)}, bf16[2,392,768]{2,1,0:T(8,128)(2,1)S(1)}, bf16[2,392,256]{2,1,0:T(8,128)(2,1)S(1)}, bf16[2,392,128]{2,1,0:T(8,128)(2,1)S(1)}) custom-call(bf16[8,14,14,256]{3,2,1,0:T(8,128)(2,1)S(1)} %maximum_maximum_fusion.tok_ref, s32[4,392,1]{2,1,0:T(8,128)S(1)} %reshape.130.lab_ref, ...), custom_call_target="tpu_custom_call" | custom-call | flops 8000000000 | bytes 8000000 | tf_op jit(solution)/shard_map/pallas_call | solution.py:143
  41.0 26.9 %shard_map.308 = (bf16[4,7,56,128]{3,2,1,0:T(8,128)(2,1)}, bf16[2,168,256]{2,1,0:T(8,128)(2,1)}, bf16[2,392,256]{2,1,0:T(8,128)(2,1)}, bf16[2,224,256]{2,1,0:T(8...) custom-call(bf16[2,168,256]{2,1,0:T(8,128)(2,1)} %collective-permute, ...), custom_call_target="tpu_custom_call" | custom-call | flops 15000000512 | bytes 20000000 | tf_op jit(solution)/shard_map/pallas_call | solution.py:398
  67.9 4.7 %collective-permute-start.4 = (bf16[2,168,256]{2,1,0:T(8,128)(2,1)}, bf16[2,168,256]{2,1,0:T(8,128)(2,1)S(1)}, u32[]{:S(2)}, u32[]{:S(2)}) collective-permute-start(bf16[2,168,256]{2,1,0:T(8,128)(2,1)} %get-tuple-element.47), channel_id=1, source_target_pairs={{0,31},{1,0},{2,1},{3,2},{4,3},{5,4},{6,5},{7,6},{8,7},{9,8},{10,9... | collective-permute-start | bytes 516104 | tf_op jit(solution)/shard_map/ppermute | solution.py:471
  72.6 1.9 constant_dynamic-update-slice_fusion.6
  75.2 1.9 constant_dynamic-update-slice_fusion.5
  77.1 2.2 constant_dynamic-update-slice_fusion.4
  79.5 11.5 %shard_map.311 = (bf16[8,7,14,256]{3,2,1,0:T(8,128)(2,1)S(1)}, f32[6,256,128]{2,1,0:T(8,128)S(1)}, f32[2,256,128]{2,1,0:T(8,128)S(1)}, f32[8,768]{1,0:T(8,128)S(1)}) custom-call(bf16[2,392,256]{2,1,0:T(8,128)(2,1)S(1)} %copy-done.22, bf16[2,392,256]{2,1,0:T(8,128)(2,1)S(1)} %copy-done.14, bf16[2,392,768]{2,1,0:T(8,128)(2,1)S(1)} %copy-done.8, ...), custom_call_target="tpu_custom_call" | custom-call | flops 20000000000 | bytes 8000000 | tf_op jit(solution)/shard_map/pallas_call | solution.py:265
  91.1 11.3 %shard_map.310 = (bf16[8,7,14,256]{3,2,1,0:T(8,128)(2,1)S(1)}, f32[6,256,128]{2,1,0:T(8,128)S(1)}, f32[2,256,128]{2,1,0:T(8,128)S(1)}, f32[8,768]{1,0:T(8,128)S(1)}) custom-call(bf16[2,392,256]{2,1,0:T(8,128)(2,1)S(1)} %pad_maximum_fusion.d_ref, bf16[2,392,256]{2,1,0:T(8,128)(2,1)S(1)} %copy-done.10, bf16[2,392,768]{2,1,0:T(8,128)(2,1)S(1)} %get-tuple-element.49.qkv_ref, ...), custom_call_target="tpu_custom_call" | custom-call | flops 20000000000 | bytes 8000000 | tf_op jit(solution)/shard_map/pallas_call | solution.py:265
  107.0 43.7 %all_to_all.20 = bf16[128,88,128]{2,1,0:T(8,128)(2,1)} all-to-all(bf16[128,88,128]{2,1,0:T(8,128)(2,1)} %bitcast.7), channel_id=1, replica_groups=mesh['tm'=4,'height'=32] {'tm','height'}, dimensions={0} | all-to-all | bytes 5767168 | tf_op jit(solution)/shard_map/all_to_all | solution.py:481
  150.7 4.7 %all-to-all-start.1 = ((bf16[4,7,56,128]{3,2,1,0:T(8,128)(2,1)}), bf16[4,7,56,128]{3,2,1,0:T(8,128)(2,1)S(1)}, u32[]{:S(2)}, u32[]{:S(2)}) async-start(bf16[4,7,56,128]{3,2,1,0:T(8,128)(2,1)} %get-tuple-element.45), calls=%async_computation.1 | async-start | bytes 802816 | tf_op jit(solution)/shard_map/all_to_all | solution.py:517
  155.4 2.3 convert_reduce_fusion
  157.7 5.9 %all-to-all-done.1.parts_ref = bf16[4,7,56,128]{3,2,1,0:T(8,128)(2,1)S(1)} async-done(((bf16[4,7,56,128]{3,2,1,0:T(8,128)(2,1)}), bf16[4,7,56,128]{3,2,1,0:T(8,128)(2,1)S(1)}, u32[]{:S(2)}, u32[]{:S(2)}) %all-to-all-start.1) | async-done | bytes 401440 | tf_op jit(solution)/shard_map/all_to_all | solution.py:517
  163.6 2.0 broadcast_in_dim.2
  165.6 5.3 %all-to-all-start.3 = ((bf16[128,88,128]{2,1,0:T(8,128)(2,1)}), bf16[128,88,128]{2,1,0:T(8,128)(2,1)}, u32[]{:S(2)}, u32[]{:S(2)}) async-start(bf16[128,88,128]{2,1,0:T(8,128)(2,1)} %broadcast_in_dim.2), calls=%async_computation.3 | async-start | bytes 5767168 | tf_op jit(solution)/shard_map/all_to_all | solution.py:484
  171.1 3.2 %collective-permute-start.6 = (bf16[4,11,14,256]{3,2,1,0:T(8,128)(2,1)S(1)}, bf16[4,11,14,256]{3,2,1,0:T(8,128)(2,1)S(1)}, u32[]{:S(2)}, u32[]{:S(2)}) collective-permute-start(bf16[4,11,14,256]{3,2,1,0:T(8,128)(2,1)S(1)} %get-tuple-element.140), channel_id=1, source_target_pairs={{0,32},{32,64},{64,96},{96,0},{1,33},{33,65},{65,97},{97,1},{2,34}... | collective-permute-start | bytes 946184 | tf_op jit(solution)/shard_map/ppermute | solution.py:471
  177.4 2.0 shard_map.309
  181.2 34.1 %collective-permute-done.7 = bf16[4,3,14,256]{3,2,1,0:T(8,128)(2,1)S(1)} collective-permute-done((bf16[4,3,14,256]{3,2,1,0:T(8,128)(2,1)S(1)}, bf16[4,3,14,256]{3,2,1,0:T(8,128)(2,1)S(1)}, u32[]{:S(2)}, u32[]{:S(2)}) %collective-permute-start.7) | collective-permute-done | bytes 86048 | tf_op jit(solution)/shard_map/ppermute | solution.py:471
  216.8 2.0 bitcast_convert_fusion
  229.3 1.8 copy.71
  231.1 2.9 %copy.78 = f32[1024,512]{1,0:T(8,128)} copy(f32[1024,512]{0,1:T(8,128)} %bitcast.55) | data formatting | bytes 4194304
  (130 shorter events, 35.7 us)
Async XLA Ops:
  0.7 13.2 %copy-start.25 = (bf16[32,7,7,128]{3,0,2,1:T(8,128)(2,1)S(1)}, bf16[32,7,7,128]{3,0,2,1:T(8,128)(2,1)}, u32[]{:S(2)}) copy-start(bf16[32,7,7,128]{3,0,2,1:T(8,128)(2,1)} %param.35) | copy-start | bytes 1204228
  0.7 21.1 %copy-start.27 = (s32[8,14,14]{2,0,1:T(8,128)S(1)}, s32[8,14,14]{2,0,1:T(8,128)}, u32[]{:S(2)}) copy-start(s32[8,14,14]{2,0,1:T(8,128)} %param.19) | copy-start | bytes 18820
  2.3 20.1 %collective-permute-start.1 = (bf16[4,11,14,256]{3,2,1,0:T(8,128)(2,1)S(1)}, bf16[4,11,14,256]{3,2,1,0:T(8,128)(2,1)S(1)}, u32[]{:S(2)}, u32[]{:S(2)}) collective-permute-start(bf16[4,11,14,256]{3,2,1,0:T(8,128)(2,1)S(1)} %copy.81), channel_id=1, source_target_pairs={{0,96},{32,0},{64,32},{96,64},{1,97},{33,1},{65,33},{97,65},{2,98}... | collective-permute-start | bytes 946184 | tf_op jit(solution)/shard_map/ppermute | solution.py:471
  4.9 17.5 %collective-permute-start.2 = (bf16[4,3,14,256]{3,2,1,0:T(8,128)(2,1)S(1)}, bf16[4,3,14,256]{3,2,1,0:T(8,128)(2,1)S(1)}, u32[]{:S(2)}, u32[]{:S(2)}) collective-permute-start(bf16[4,3,14,256]{3,2,1,0:T(8,128)(2,1)S(1)} %copy.82), channel_id=1, source_target_pairs={{0,127},{1,96},{2,97},{3,98},{4,99},{5,100},{6,101},{7,102},{8,103... | collective-permute-start | bytes 258056 | tf_op jit(solution)/shard_map/ppermute | solution.py:471
  13.6 8.8 %collective-permute-start = (bf16[4,3,14,256]{3,2,1,0:T(8,128)(2,1)S(1)}, bf16[4,3,14,256]{3,2,1,0:T(8,128)(2,1)S(1)}, u32[]{:S(2)}, u32[]{:S(2)}) collective-permute-start(bf16[4,3,14,256]{3,2,1,0:T(8,128)(2,1)S(1)} %copy.80), channel_id=1, source_target_pairs={{0,31},{1,0},{2,1},{3,2},{4,3},{5,4},{6,5},{7,6},{8,7},{9,8},{10,9... | collective-permute-start | bytes 258056 | tf_op jit(solution)/shard_map/ppermute | solution.py:471
  14.8 7.8 %copy-start.5 = (f32[256]{0:T(256)S(1)}, f32[256]{0:T(256)}, u32[]{:S(2)}) copy-start(f32[256]{0:T(256)} %gain_ref.7) | copy-start | bytes 3076
  14.8 7.8 %copy-start.6 = (f32[256]{0:T(256)S(1)}, f32[256]{0:T(256)}, u32[]{:S(2)}) copy-start(f32[256]{0:T(256)} %bias_ref.7) | copy-start | bytes 3076
  16.8 24.1 %all-to-all-start = ((bf16[4,7,56,128]{3,2,1,0:T(8,128)(2,1)}), bf16[4,7,56,128]{3,2,1,0:T(8,128)(2,1)}, u32[]{:S(2)}, u32[]{:S(2)}) async-start(bf16[4,7,56,128]{3,2,1,0:T(8,128)(2,1)} %shard_map.307), calls=%async_computation | async-start | bytes 802816 | tf_op jit(solution)/shard_map/all_to_all | solution.py:506
  30.4 10.6 %collective-permute-start.3 = (bf16[2,168,256]{2,1,0:T(8,128)(2,1)}, bf16[2,168,256]{2,1,0:T(8,128)(2,1)}, u32[]{:S(2)}, u32[]{:S(2)}) collective-permute-start(bf16[2,168,256]{2,1,0:T(8,128)(2,1)} %slice.107), channel_id=1, source_target_pairs={{0,1},{1,2},{2,3},{3,4},{4,5},{5,6},{6,7},{7,8},{8,9},{9,10},{10,1... | collective-permute-start | bytes 516104 | tf_op jit(solution)/shard_map/ppermute | solution.py:471
  67.8 11.5 %copy-start.8 = (bf16[2,392,768]{2,1,0:T(8,128)(2,1)S(1)}, bf16[2,392,768]{2,1,0:T(8,128)(2,1)}, u32[]{:S(2)}) copy-start(bf16[2,392,768]{2,1,0:T(8,128)(2,1)} %copy-done.7) | copy-start | bytes 3612676
  67.8 11.5 %copy-start.14 = (bf16[2,392,256]{2,1,0:T(8,128)(2,1)S(1)}, bf16[2,392,256]{2,1,0:T(8,128)(2,1)}, u32[]{:S(2)}) copy-start(bf16[2,392,256]{2,1,0:T(8,128)(2,1)} %copy-done.13) | copy-start | bytes 1204228
  67.9 11.5 %copy-start.16 = (bf16[2,392,256]{2,1,0:T(8,128)(2,1)S(1)}, bf16[2,392,256]{2,1,0:T(8,128)(2,1)}, u32[]{:S(2)}) copy-start(bf16[2,392,256]{2,1,0:T(8,128)(2,1)} %copy-done.15) | copy-start | bytes 1204228
  67.9 11.5 %copy-start.21 = (bf16[2,392,128]{2,1,0:T(8,128)(2,1)S(1)}, bf16[2,392,128]{2,1,0:T(8,128)(2,1)}, u32[]{:S(2)}) copy-start(bf16[2,392,128]{2,1,0:T(8,128)(2,1)} %copy-done.20) | copy-start | bytes 602116
  67.9 11.5 %copy-start.22 = (bf16[2,392,256]{2,1,0:T(8,128)(2,1)S(1)}, bf16[2,392,256]{2,1,0:T(8,128)(2,1)}, u32[]{:S(2)}) copy-start(bf16[2,392,256]{2,1,0:T(8,128)(2,1)} %get-tuple-element.53.d_ref) | copy-start | bytes 1204228
  67.9 23.2 %collective-permute-start.4 = (bf16[2,168,256]{2,1,0:T(8,128)(2,1)}, bf16[2,168,256]{2,1,0:T(8,128)(2,1)S(1)}, u32[]{:S(2)}, u32[]{:S(2)}) collective-permute-start(bf16[2,168,256]{2,1,0:T(8,128)(2,1)} %get-tuple-element.47), channel_id=1, source_target_pairs={{0,31},{1,0},{2,1},{3,2},{4,3},{5,4},{6,5},{7,6},{8,7},{9,8},{10,9... | collective-permute-start | bytes 516104 | tf_op jit(solution)/shard_map/ppermute | solution.py:471
  79.4 11.7 %copy-start.26 = (bf16[2,224,256]{2,1,0:T(8,128)(2,1)S(1)}, bf16[2,224,256]{2,1,0:T(8,128)(2,1)}, u32[]{:S(2)}) copy-start(bf16[2,224,256]{2,1,0:T(8,128)(2,1)} %get-tuple-element.46) | copy-start | bytes 688132
  79.4 11.7 %copy-start.10 = (bf16[2,392,256]{2,1,0:T(8,128)(2,1)S(1)}, bf16[2,392,256]{2,1,0:T(8,128)(2,1)}, u32[]{:S(2)}) copy-start(bf16[2,392,256]{2,1,0:T(8,128)(2,1)} %copy-done.9) | copy-start | bytes 1204228
  79.4 11.7 %copy-start.12 = (bf16[2,392,256]{2,1,0:T(8,128)(2,1)S(1)}, bf16[2,392,256]{2,1,0:T(8,128)(2,1)}, u32[]{:S(2)}) copy-start(bf16[2,392,256]{2,1,0:T(8,128)(2,1)} %copy-done.11) | copy-start | bytes 1204228
  79.4 11.7 %copy-start.19 = (bf16[2,392,128]{2,1,0:T(8,128)(2,1)S(1)}, bf16[2,392,128]{2,1,0:T(8,128)(2,1)}, u32[]{:S(2)}) copy-start(bf16[2,392,128]{2,1,0:T(8,128)(2,1)} %copy-done.18) | copy-start | bytes 602116
  150.7 12.9 %all-to-all-start.1 = ((bf16[4,7,56,128]{3,2,1,0:T(8,128)(2,1)}), bf16[4,7,56,128]{3,2,1,0:T(8,128)(2,1)S(1)}, u32[]{:S(2)}, u32[]{:S(2)}) async-start(bf16[4,7,56,128]{3,2,1,0:T(8,128)(2,1)} %get-tuple-element.45), calls=%async_computation.1 | async-start | bytes 802816 | tf_op jit(solution)/shard_map/all_to_all | solution.py:517
  165.6 51.3 %all-to-all-start.3 = ((bf16[128,88,128]{2,1,0:T(8,128)(2,1)}), bf16[128,88,128]{2,1,0:T(8,128)(2,1)}, u32[]{:S(2)}, u32[]{:S(2)}) async-start(bf16[128,88,128]{2,1,0:T(8,128)(2,1)} %broadcast_in_dim.2), calls=%async_computation.3 | async-start | bytes 5767168 | tf_op jit(solution)/shard_map/all_to_all | solution.py:484
  171.1 44.3 %collective-permute-start.6 = (bf16[4,11,14,256]{3,2,1,0:T(8,128)(2,1)S(1)}, bf16[4,11,14,256]{3,2,1,0:T(8,128)(2,1)S(1)}, u32[]{:S(2)}, u32[]{:S(2)}) collective-permute-start(bf16[4,11,14,256]{3,2,1,0:T(8,128)(2,1)S(1)} %get-tuple-element.140), channel_id=1, source_target_pairs={{0,32},{32,64},{64,96},{96,0},{1,33},{33,65},{65,97},{97,1},{2,34}... | collective-permute-start | bytes 946184 | tf_op jit(solution)/shard_map/ppermute | solution.py:471
  174.3 41.0 %collective-permute-start.7 = (bf16[4,3,14,256]{3,2,1,0:T(8,128)(2,1)S(1)}, bf16[4,3,14,256]{3,2,1,0:T(8,128)(2,1)S(1)}, u32[]{:S(2)}, u32[]{:S(2)}) collective-permute-start(bf16[4,3,14,256]{3,2,1,0:T(8,128)(2,1)S(1)} %get-tuple-element.147), channel_id=1, source_target_pairs={{0,1},{1,2},{2,3},{3,4},{4,5},{5,6},{6,7},{7,8},{8,9},{9,10},{10,1... | collective-permute-start | bytes 258056 | tf_op jit(solution)/shard_map/ppermute | solution.py:471
  175.8 39.5 %collective-permute-start.5 = (bf16[4,3,14,256]{3,2,1,0:T(8,128)(2,1)S(1)}, bf16[4,3,14,256]{3,2,1,0:T(8,128)(2,1)S(1)}, u32[]{:S(2)}, u32[]{:S(2)}) collective-permute-start(bf16[4,3,14,256]{3,2,1,0:T(8,128)(2,1)S(1)} %get-tuple-element.146), channel_id=1, source_target_pairs={{0,33},{1,34},{2,35},{3,36},{4,37},{5,38},{6,39},{7,40},{8,41},{9,... | collective-permute-start | bytes 258056 | tf_op jit(solution)/shard_map/ppermute | solution.py:471
  (17 other events, 62.4 us)

commit v2 on v1

v2 whole, which is shorter than its diff:
```python
import functools
import math

import jax
import jax.numpy as jnp
from jax import lax
from jax.experimental import pallas as pl
from jax.experimental.pallas import tpu as pltpu
from jax.sharding import PartitionSpec as P

F32 = jnp.float32
BF16 = jnp.bfloat16
NORM_EPS = 1e-05
DIM = 256
CELLS = 392
TILES = 49
FAR = 2.0**100
SCORE_SCALE = math.log2(math.e) / math.sqrt(32.0)
MIB = 1 << 20


def dot(a, b):
    return lax.dot_general(a, b, (((1,), (0,)), ((), ())), preferred_element_type=F32)


def dot_nt(a, b):
    return lax.dot_general(a, b, (((1,), (1,)), ((), ())), preferred_element_type=F32)


def dot_tn(a, b):
    return lax.dot_general(a, b, (((0,), (0,)), ((), ())), preferred_element_type=F32)


def row(ref):
    return ref[...].reshape(1, -1)


def norm_stats(x):
    average = jnp.mean(x, -1, keepdims=True)
    centred = x - average
    rstd = lax.rsqrt(jnp.mean(centred * centred, -1, keepdims=True) + NORM_EPS)
    return centred * rstd, rstd


def norm_back(dxhat, xhat, rstd):
    first = jnp.mean(dxhat, -1, keepdims=True)
    second = jnp.mean(dxhat * xhat, -1, keepdims=True)
    return (dxhat - first - xhat * second) * rstd


def lanes(rows):
    return lax.broadcasted_iota(jnp.int32, (rows, 128), 1)


def head_mask(index):
    return (lanes(1) // 32 == index).astype(BF16)


def three_parts(value, lane, start):
    high = value.astype(BF16).astype(F32)
    middle = (value - high).astype(BF16).astype(F32)
    low = value - high - middle
    return jnp.where(lane < start + 8, high, jnp.where(lane < start + 16, middle, low))


def attend_kernel(
    tok_ref, lab_ref, gain_ref, bias_ref, wi_ref, bi_ref, wo_ref, bo_ref,
    res_ref, x_ref, qkv_ref, ctx_ref, eq_ref, field,
):
    win = pl.program_id(0)

    @pl.when(win == 0)
    def spread():
        for f in range(8):
            for r in range(7):
                start = (f * 7 + r) * 16
                cells = tok_ref[f, r].astype(F32)
                for half in range(2):
                    field[half, start : start + 14, :] = cells[:, 128 * half : 128 * half + 128]

    def window():
        parts = []
        for wi in range(7):
            for wj in range(7):
                column = lax.rem(win * 7 + wj + 3, 14)
                parts.append(
                    jnp.concatenate(
                        [field[s, pl.ds(wi * 16 + column, 8, stride=112), :] for s in range(2)],
                        1,
                    )
                )
        x = jnp.concatenate(parts, 0)
        x_ref[0] = x.astype(BF16)
        xhat, _ = norm_stats(x)
        normed = (xhat * row(gain_ref) + row(bias_ref)).astype(BF16)
        packed = dot(normed, wi_ref[...]) + row(bi_ref)
        q = (packed[:, 0:256] * SCORE_SCALE).astype(BF16)
        k = packed[:, 256:512].astype(BF16)
        v = packed[:, 512:768]
        vb = v.astype(BF16)
        vs = (v * (2.0**-12)).astype(BF16)
        qkv_ref[0, :, 0:256] = q
        qkv_ref[0, :, 256:512] = k
        qkv_ref[0, :, 512:768] = vb
        label = lab_ref[0]
        lane = lanes(CELLS)
        same = lane == label
        eq32 = jnp.where(same | (lane == 27), 1.0, 0.0)
        eq = eq32.astype(BF16)
        ek = jnp.where(
            lane < 27, jnp.where(same, 0.0, -FAR), jnp.where(lane == 27, -1.0, 0.0)
        ).astype(BF16)
        ones = jnp.ones((CELLS, 128), BF16)
        sums = jnp.ones((CELLS, 128), F32)
        halves = []
        for t in range(2):
            qt = q[:, 128 * t : 128 * t + 128]
            kaug = jnp.concatenate([k[:, 128 * t : 128 * t + 128], ek], 1)
            vaug = jnp.concatenate([vs[:, 128 * t : 128 * t + 128], ones], 1)
            half = jnp.zeros((CELLS, 128), F32)
            for hh in range(4):
                h = 4 * t + hh
                qaug = jnp.concatenate([qt * head_mask(hh), eq], 1)
                p = jnp.exp2(dot_nt(qaug, kaug)).astype(BF16)
                pv = dot(p, vaug)
                total = pv[:, 128:256]
                half = jnp.where(lane // 32 == hh, pv[:, 0:128] * (4096.0 / total), half)
                sums = jnp.where((lane >= 32) & (lane < 56) & (lane % 8 == h), total, sums)
            halves.append(half)
        ctx = jnp.concatenate(halves, 1).astype(BF16)
        ctx_ref[0] = ctx
        minus = three_parts(-jnp.log2(sums), lane, 32)
        eq_ref[0] = jnp.where((lane >= 32) & (lane < 56), minus, eq32).astype(BF16)
        attended = (dot(ctx, wo_ref[...]) + row(bo_ref)).astype(BF16)
        res_ref[0] = (x + attended.astype(F32)).astype(BF16)

    window()


def on_device(kernel, outs, ins, scratch, limit, flops, steps=1, in_blocks=None, out_blocks=None):
    def specs(arrays, blocks):
        found = [pl.BlockSpec(a, lambda i, n=len(a): (0,) * n) for a in arrays]
        for at, how in (blocks or {}).items():
            found[at] = pl.BlockSpec(*how) if how else pl.BlockSpec(memory_space=pl.ANY)
        return found

    return pl.pallas_call(
        kernel,
        grid=(steps,),
        in_specs=specs([a.shape for a in ins], in_blocks),
        out_specs=specs([a for a, _ in outs], out_blocks),
        out_shape=[pltpu.HBM(s, t) for s, t in outs],
        scratch_shapes=[pltpu.SemaphoreType.DMA(s) if t is None else pltpu.VMEM(s, t) for s, t in scratch],
        compiler_params=pltpu.CompilerParams(vmem_limit_bytes=limit * MIB),
        cost_estimate=pl.CostEstimate(flops=flops, bytes_accessed=4 * 10**6, transcendentals=0),
    )(*[pltpu.with_memory_space_constraint(a, pltpu.HBM) for a in ins])


def by_window(rows, width):
    return (1, rows, width), lambda i: (i, 0, 0)


def attend(row_win, *ins):
    widths = [256, 256, 768, 256, 128]
    outs = [((2, CELLS, width), BF16) for width in widths]
    in_blocks = {
        0: ((8, 7, 14, 256), lambda i: (0, row_win, 0, 0)),
        1: ((1, CELLS, 1), lambda i: (2 * row_win + i, 0, 0)),
    }
    out_blocks = {n: by_window(CELLS, width) for n, width in enumerate(widths)}
    scratch = [((2, 896, 128), F32)]
    return on_device(attend_kernel, outs, ins, scratch, 40, 4 * 10**9, 2, in_blocks, out_blocks)


def attend_back_kernel(last, *refs):
    if last:
        (d_ref, below_ref, x_ref, qkv_ref, ctx_ref, eq_ref, lab_ref, gain_ref, bias_ref, wi_ref, wo_ref,
         dwi_ref, dwo_ref, vec_ref, post_ref, out_ref, slab_ref, field, dwi, dwo, vec) = refs
    else:
        (d_ref, x_ref, qkv_ref, ctx_ref, eq_ref, lab_ref, gain_ref, bias_ref, wi_ref, wo_ref,
         out_ref, dwi, dwo, vec, field) = refs

    win = pl.program_id(0)

    @pl.when(win == 0)
    def start():
        dwi[...] = dwi_ref[...] if last else jnp.zeros_like(dwi)
        dwo[...] = dwo_ref[...] if last else jnp.zeros_like(dwo)
        vec[...] = vec_ref[...] if last else jnp.zeros_like(vec)

    def window():
        d = jnp.concatenate([d_ref[0], below_ref[0]], 0) if last else d_ref[0]
        d32 = d.astype(F32)
        ctx = ctx_ref[0]
        dwo[...] += dot_tn(ctx, d)
        vec[3:4, 0:256] += jnp.sum(d32, 0, keepdims=True)
        dctx = dot_nt(d, wo_ref[...]).astype(BF16)
        product = dctx.astype(F32) * ctx.astype(F32)
        high = product.astype(BF16)
        low = (product - high.astype(F32)).astype(BF16)
        picks_r = lax.broadcasted_iota(jnp.int32, (256, 128), 0) // 32
        picks_c = lax.broadcasted_iota(jnp.int32, (256, 128), 1)
        picks = ((picks_c < 24) & (picks_c % 8 == picks_r)).astype(BF16)
        lane = lanes(CELLS)
        delta = three_parts(-(dot(high, picks) + dot(low, picks)), lane, 0)
        dd = jnp.where(lane < 24, delta, 0.0).astype(BF16)
        eq = eq_ref[0]
        same = lane == lab_ref[0]
        ek = jnp.where(lane < 27, jnp.where(same, 0.0, -FAR), jnp.where(lane == 27, -1.0, 0.0))
        lane1 = lanes(1)
        dqs, dks, dvs = [], [], []
        for t in range(2):
            cols = slice(128 * t, 128 * t + 128)
            qt = qkv_ref[0, :, 128 * t : 128 * t + 128]
            kt = qkv_ref[0, :, 256 + 128 * t : 256 + 128 * t + 128]
            vt = qkv_ref[0, :, 512 + 128 * t : 512 + 128 * t + 128]
            dot_t = dctx[:, cols]
            qaug = jnp.concatenate([qt, eq], 1)
            daug = jnp.concatenate([dot_t, dd], 1)
            ktt = jnp.transpose(kt.astype(F32)).astype(BF16)
            dk = jnp.zeros((CELLS, 128), F32)
            dv = jnp.zeros((CELLS, 128), F32)
            dqt = []
            for hh in range(4):
                h = 4 * t + hh
                mask = head_mask(hh)
                picked = (lane1 >= 32) & (lane1 < 56) & (lane1 % 8 == h)
                kaug = jnp.concatenate([kt * mask, jnp.where(picked, 1.0, ek).astype(BF16)], 1)
                tail = jnp.where((lane < 24) & (lane % 8 == h), 1.0, 0.0).astype(BF16)
                vaug = jnp.concatenate([vt * mask, tail], 1)
                p = jnp.exp2(dot_nt(kaug, qaug))
                ds = (p * dot_nt(vaug, daug)).astype(BF16)
                dv = dv + dot(p.astype(BF16), dot_t * mask)
                dk = dk + dot(ds, qt * mask)
                dqt.append(dot(ktt[32 * hh : 32 * hh + 32, :], ds))
            dqs.append(jnp.transpose(jnp.concatenate(dqt, 0)))
            dks.append(dk)
            dvs.append(dv)
        dpacked32 = jnp.concatenate(
            [d_q * (1.0 / math.sqrt(32.0)) for d_q in dqs]
            + [d_k * math.log(2.0) for d_k in dks]
            + dvs,
            1,
        )
        dpacked = dpacked32.astype(BF16)
        vec[2:3, :] += jnp.sum(dpacked32, 0, keepdims=True)
        x = x_ref[0].astype(F32)
        xhat, rstd = norm_stats(x)
        gain = row(gain_ref)
        normed = (xhat * gain + row(bias_ref)).astype(BF16)
        dwi[...] += dot_tn(normed, dpacked)
        dnormed = dot_nt(dpacked, wi_ref[...]).astype(BF16).astype(F32)
        vec[0:1, 0:256] += jnp.sum(dnormed * xhat, 0, keepdims=True)
        vec[1:2, 0:256] += jnp.sum(dnormed, 0, keepdims=True)
        dx = norm_back(dnormed * gain, xhat, rstd).astype(BF16).astype(F32) + d32
        for wi in range(7):
            for wj in range(7):
                column = lax.rem(win * 7 + wj + 3, 14)
                at = (wi * 7 + wj) * 8
                for s in range(2):
                    field[s, pl.ds(wi * 16 + column, 8, stride=112), :] = dx[at : at + 8, 128 * s : 128 * s + 128]

    window()

    @pl.when(win == 1)
    def finish():
        finish_back(last, refs, out_ref, field, dwi, dwo, vec)


def finish_back(last, refs, out_ref, field, dwi, dwo, vec):
    if last:
        post_ref, slab_ref = refs[14], refs[16]
    for f in range(8):
        for r in range(7):
            start = (f * 7 + r) * 16
            halves = [field[s, start : start + 14, :] for s in range(2)]
            out_ref[f, r] = jnp.concatenate(halves, 1).astype(BF16)
    if last:
        for n in range(128):
            rows = slice(16 * (n % 16), 16 * (n % 16) + 16)
            first = 128 * (n // 16)
            source = dwi[rows, first : first + 128] if n < 96 else dwo[rows, first - 768 : first - 640]
            slab_ref[n, 0:16, :] = source.astype(BF16)
        tiles = [vec[:, 128 * c : 128 * c + 128] for c in range(6)]
        tiles += [post_ref[:, 128 * c : 128 * c + 128] for c in range(8)]
        for n in range(128):
            tile = tiles[n] if n < 14 else jnp.zeros((8, 128), F32)
            slab_ref[n, 16:24, :] = tile.astype(BF16)


LATE = 24
EARLY = 64


def attend_back(row_win, given, saved, labels, params, sums):
    last = row_win == 1
    sum_shapes = [((256, 768), F32), ((256, 256), F32), ((8, 768), F32)]
    outs = [((8, 7, 14, 256), BF16)] + ([((128, LATE, 128), BF16)] if last else sum_shapes)
    ins = tuple(given) + tuple(saved) + (labels,) + tuple(params) + tuple(sums)
    scratch = [((2, 896, 128), F32)] + (sum_shapes if last else [])
    in_blocks = {n: by_window(*a.shape[1:]) for n, a in enumerate(tuple(given) + tuple(saved))}
    in_blocks[len(in_blocks)] = ((1, CELLS, 1), lambda i: (2 * row_win + i, 0, 0))
    kernel = functools.partial(attend_back_kernel, last)
    return on_device(kernel, outs, ins, scratch, 40, 6 * 10**9, 2, in_blocks)


def gelu_pair(v):
    half_square = jnp.exp2(v * v * (-0.5 * math.log2(math.e)))
    t = 1.0 / (1.0 + jnp.abs(v) * (0.3275911 * math.sqrt(0.5)))
    poly = t * (0.5 * 0.254829592 + t * (0.5 * -0.284496736 + t * (0.5 * 1.421413741 + t * (0.5 * -1.453152027 + t * (0.5 * 1.061405429)))))
    tail = poly * half_square
    phi = jnp.where(v >= 0.0, 1.0 - tail, tail)
    return v * phi, phi + v * half_square * (1.0 / math.sqrt(2.0 * math.pi))


QUADRANTS = ((0, 0), (1, 0), (0, 1), (1, 1))


def tile_start(r, c):
    s = (c - 3) % 14
    return ((s // 7) * 14 + r) * 56 + (s % 7) * 8


KEPT = ((256, 224), (1024, 224), (256, 224), (1024, 224), (1024, 64), (512, 64))


def post_chunks(first, count, field, params, merged_ref, cot_ref, kept, vec):
    sg_ref, sb_ref, we_ref, be_ref, wr_ref, br_ref, mg_ref, mb_ref, wm_ref = params
    sn_all, hid_all, dbo_all, dpre_all, mn_all, dm_all = kept
    sg, sb, be, br = row(sg_ref), row(sb_ref), row(be_ref), row(br_ref)

    def chunk(i, carry):
        starts = []
        for rp, cp in QUADRANTS:
            for j in range(7):
                starts.append(pl.multiple_of(tile_start(0, 2 * j + cp) + (2 * i + rp) * 56, 8))
        x = jnp.concatenate([field[pl.ds(s, 8), :] for s in starts], 0)
        xhat, rstd = norm_stats(x)
        sn = (xhat * sg + sb).astype(BF16)
        here = pl.multiple_of(i * 224, 16)
        sn_all[pl.ds(here, 224), :] = sn
        hidden, slope = gelu_pair(dot(sn, we_ref[...]) + be)
        hidden = hidden.astype(BF16)
        hid_all[pl.ds(here, 224), :] = hidden
        out = (x + dot(hidden, wr_ref[...]) + br).astype(BF16).astype(F32)
        gathered = jnp.concatenate([out[56 * q : 56 * q + 56, :] for q in range(4)], 1)
        mhat, mrstd = norm_stats(gathered)
        mg = row(mg_ref)
        mn = mhat * mg + row(mb_ref)
        merged = dot(mn.astype(BF16), wm_ref[...])
        pad = pl.multiple_of(i * 64, 64)
        mn_all[pl.ds(pad, 64), :] = jnp.concatenate([mn, jnp.zeros((8, 1024), F32)], 0).astype(BF16)
        for s in range(4):
            merged_ref[s, i] = merged[:, 128 * s : 128 * s + 128].astype(BF16)
        dm32 = jnp.concatenate([cot_ref[s, i].astype(F32) for s in range(4)], 1)
        dm_all[pl.ds(pad, 64), :] = jnp.concatenate([dm32, jnp.zeros((8, 512), F32)], 0).astype(BF16)
        dmn = dot_nt(dm32.astype(BF16), wm_ref[...]).astype(BF16).astype(F32)
        vec[4:5, :] += jnp.sum(dmn * mhat, 0, keepdims=True)
        vec[5:6, :] += jnp.sum(dmn, 0, keepdims=True)
        dgathered = norm_back(dmn * mg, mhat, mrstd)
        dbo32 = jnp.concatenate([dgathered[:, 256 * q : 256 * q + 256] for q in range(4)], 0)
        dbo = dbo32.astype(BF16)
        dbo32 = dbo.astype(F32)
        dbo_all[pl.ds(here, 224), :] = dbo
        vec[3:4, 0:256] += jnp.sum(dbo32, 0, keepdims=True)
        dpre32 = dot_nt(dbo, wr_ref[...]) * slope
        vec[2:3, :] += jnp.sum(dpre32, 0, keepdims=True)
        dpre = dpre32.astype(BF16)
        dpre_all[pl.ds(here, 224), :] = dpre
        dsn = dot_nt(dpre, we_ref[...]).astype(BF16).astype(F32)
        vec[0:1, 0:256] += jnp.sum(dsn * xhat, 0, keepdims=True)
        vec[1:2, 0:256] += jnp.sum(dsn, 0, keepdims=True)
        dx = dbo32 + norm_back(dsn * sg, xhat, rstd)
        for n, s in enumerate(starts):
            field[pl.ds(s, 8), :] = dx[8 * n : 8 * n + 8, :]
        return carry

    lax.fori_loop(first, first + count, chunk, 0)


def post_first_kernel(above_ref, res0_ref, cot_ref, *refs):
    params, (merged_ref, dabove_ref, d0_ref), kept = refs[:9], refs[9:12], refs[12:18]
    vec, field = refs[18:]
    for wc in range(2):
        field[wc * 784 : wc * 784 + 168, :] = above_ref[wc].astype(F32)
        field[wc * 784 + 168 : wc * 784 + 224, :] = res0_ref[wc, 0:56, :].astype(F32)
    vec[...] = jnp.zeros_like(vec)
    post_chunks(0, 2, field, params, merged_ref, cot_ref, kept, vec)
    for wc in range(2):
        dabove_ref[wc] = field[wc * 784 : wc * 784 + 168, :].astype(BF16)
        d0_ref[wc] = field[wc * 784 + 168 : wc * 784 + 224, :]


def post_second_kernel(res0_ref, res1_ref, cot_ref, *refs):
    params, (vec_in_ref, merged_in_ref, d0_in_ref), brought = refs[:9], refs[9:12], refs[12:18]
    (merged_ref, d0_ref, d1_ref, slab_ref, vec), field, kept, sems = refs[18:23], refs[23], refs[24:30], refs[30]
    copies = []
    for n, (source, target) in enumerate(zip(brought, kept, strict=True)):
        rows = source.shape[0]
        copies.append(pltpu.make_async_copy(source, target.at[0:rows], sems.at[n]))
        copies[-1].start()
    for wc in range(2):
        base = wc * 784
        field[base + 168 : base + 560, :] = res0_ref[wc].astype(F32)
        field[base + 560 : base + 784, :] = res1_ref[wc, 0:224, :].astype(F32)
    vec[...] = vec_in_ref[...]
    merged_ref[:, 0:2] = merged_in_ref[...]
    post_chunks(2, 5, field, params, merged_ref, cot_ref, kept, vec)
    for wc in range(2):
        base = wc * 784
        field[base + 168 : base + 224, :] = d0_in_ref[wc]
        d0_ref[wc] = field[base + 168 : base + 560, :].astype(BF16)
        d1_ref[wc] = field[base + 560 : base + 784, :].astype(BF16)
    for copy in copies:
        copy.wait()
    sn_all, hid_all, dbo_all, dpre_all, mn_all, dm_all = kept
    dwe = dot_tn(sn_all[...], dpre_all[...])
    for s in range(8):
        slab_ref[256 * s : 256 * s + 256, :] = dwe[:, 128 * s : 128 * s + 128].astype(BF16)
    dwr = dot_tn(hid_all[...], dbo_all[...])
    for s in range(2):
        start = 2048 + 1024 * s
        slab_ref[start : start + 1024, :] = dwr[:, 128 * s : 128 * s + 128].astype(BF16)
    dwm = dot_tn(mn_all[...], dm_all[...])
    for s in range(4):
        start = 4096 + 1024 * s
        slab_ref[start : start + 1024, :] = dwm[:, 128 * s : 128 * s + 128].astype(BF16)


def kept_shapes(chunks):
    return [((chunks * rows, width), BF16) for width, rows in KEPT]


def post_first(above, res0, cot, params):
    outs = [((4, 2, 56, 128), BF16), ((2, 168, 256), BF16), ((2, 56, 256), F32)]
    outs += kept_shapes(2) + [((8, 1024), F32)]
    in_blocks = {
        1: ((2, 64, 256), lambda i: (0, 0, 0)),
        2: ((4, 2, 56, 128), lambda i: (0, 0, 0, 0)),
    }
    scratch = [((1568, 256), F32)]
    ins = (above, res0, cot) + params
    return on_device(post_first_kernel, outs, ins, scratch, 50, 4 * 10**9, 1, in_blocks)


def post_second(res0, res1, cot, params, vec, merged, d0, brought):
    outs = [
        ((4, 7, 56, 128), BF16),
        ((2, CELLS, 256), BF16),
        ((2, 224, 256), BF16),
        ((8192, 128), BF16),
        ((8, 1024), F32),
    ]
    scratch = [((1568, 256), F32)] + kept_shapes(7) + [((6,), None)]
    ins = (res0, res1, cot) + params + (vec, merged, d0) + tuple(brought)
    in_blocks = {n: None for n in range(15, 21)}
    return on_device(post_second_kernel, outs, ins, scratch, 50, 11 * 10**9, 1, in_blocks)


def split_frames_kernel(cot_ref, out_ref, field):
    for f in range(36):
        for i in range(7):
            start = (f * 7 + i) * 8
            field[start : start + 7, :] = cot_ref[f % 32, i].astype(F32)
    for d in range(4):
        for i in range(7):
            tiles = [
                field[pl.ds(((8 * d + 4) * 7 + i) * 8 + j, 8, stride=56), :] for j in range(7)
            ]
            out_ref[d, i] = jnp.concatenate(tiles, 0).astype(BF16)


def split_frames(cotangent):
    outs = [((4, 7, 56, 128), BF16)]
    return on_device(split_frames_kernel, outs, (cotangent,), [((2016, 128), F32)], 16, 10**6)[0]


def join_frames_kernel(p0_ref, p1_ref, p2_ref, p3_ref, out_ref, field):
    me = lax.axis_index("tm")
    for back, ref in enumerate((p0_ref, p1_ref, p2_ref, p3_ref)):
        source = lax.rem(me + 4 - back, 4)
        for i in range(7):
            tiles = ref[i].astype(F32)
            for j in range(7):
                field[pl.ds(source * 448 + 224 + i * 8 + j, 8, stride=56), :] = tiles[8 * j : 8 * j + 8]
    for f in range(32):
        source = f + 32 if f < 4 else f
        for i in range(7):
            start = (source * 7 + i) * 8
            out_ref[f, i] = field[start : start + 7, :].astype(BF16)


def join_frames(*parts):
    outs = [((32, 7, 7, 128), BF16)]
    return on_device(join_frames_kernel, outs, parts, [((2016, 128), F32)], 16, 10**6)[0]


def moved(value, axis, steps):
    sizes = [lax.axis_size(a) for a in axis]
    total = math.prod(sizes)
    pairs = []
    for source in range(total):
        if len(axis) == 1:
            pairs.append((source, (source + steps) % total))
        else:
            t, h = divmod(source, sizes[1])
            pairs.append((source, ((t + steps) % sizes[0]) * sizes[1] + (h + steps) % sizes[1]))
    return lax.ppermute(value, axis if len(axis) > 1 else axis[0], pairs)


TM = ("tm",)
ROWS = ("height",)
BOTH = ("tm", "height")


def total_of(parts_ref, rows, factor):
    total = parts_ref[0, rows, :].astype(F32)
    for n in range(1, 128):
        total = total + parts_ref[n, rows, :].astype(F32)
    return (total * factor).astype(BF16)


def sum_early_kernel(factor, parts_ref, late_ref, out_ref, total):
    @pl.when(pl.program_id(0) == 0)
    def start():
        total[...] = total_of(parts_ref, slice(0, EARLY), factor)

    core = lax.rem(pl.program_id(0), 2)
    half = total[pl.ds(pl.multiple_of(core * HALF, HALF), HALF), :]
    for n in range(32):
        out_ref[n, 0:HALF, :] = half
        out_ref[n, HALF : HALF + LATE, :] = late_ref[n]


HALF = EARLY // 2


def sum_early(factor, *ins):
    outs = [((128, HALF + LATE, 128), BF16)]
    scratch = [((EARLY, 128), BF16)]
    part = lambda rows: ((32, rows, 128), lambda i: (i, 0, 0))
    kernel = functools.partial(sum_early_kernel, factor)
    return on_device(kernel, outs, ins, scratch, 24, 10**6, 4, {1: part(LATE)}, {0: part(HALF + LATE)})[0]


def sum_late_kernel(factor, parts_ref, out_ref):
    total = total_of(parts_ref, slice(HALF, HALF + LATE), factor)
    for n in range(128):
        out_ref[n] = total


def exchange(parts):
    return lax.all_to_all(parts, BOTH, 0, 0, tiled=True)


def unpack_early_kernel(own_ref, other_ref, dwe_ref, dwr_ref, dwm_ref):
    core = lax.rem(lax.axis_index("tm"), 2)
    for ref, place in ((own_ref, core), (other_ref, 1 - core)):
        shift = pl.multiple_of(place * HALF, HALF)
        for n in range(128):
            tile = ref[n, 0:HALF, :].astype(F32)
            if n < 32:
                rows, c, out = EARLY * (n % 4), n // 4, dwe_ref
            elif n < 64:
                rows, c, out = EARLY * (n % 16), n // 16 - 2, dwr_ref
            else:
                rows, c, out = EARLY * (n % 16), n // 16 - 4, dwm_ref
            out[pl.ds(rows + shift, HALF), 128 * c : 128 * c + 128] = tile


VECTORS = ((0, 0, 2), (1, 0, 2), (2, 0, 6), (3, 0, 2), (0, 6, 2), (1, 6, 2), (2, 6, 8), (3, 6, 2), (4, 6, 8), (5, 6, 8))


def unpack_late_kernel(slab_ref, dwi_ref, dwo_ref, *vec_refs):
    for n in range(128):
        tile = slab_ref[n, 0:16, :].astype(F32)
        rows = slice(16 * (n % 16), 16 * (n % 16) + 16)
        first = 128 * (n // 16)
        if n < 96:
            dwi_ref[rows, first : first + 128] = tile
        else:
            dwo_ref[rows, first - 768 : first - 640] = tile
    tiles = [slab_ref[n, 16:24, :].astype(F32) for n in range(14)]
    for (at, first, count), ref in zip(VECTORS, vec_refs, strict=True):
        rows = [tiles[first + c][at : at + 1, :] for c in range(count)]
        ref[...] = jnp.concatenate(rows, 1).reshape(128 * count)


def unpack(kernel, slabs, shapes):
    return on_device(kernel, [(s, F32) for s in shapes], slabs, [], 32, 10**6)


def rotate_frames(parts, order):
    me = lax.axis_index("tm")
    taken = [lax.dynamic_index_in_dim(parts, lax.rem(me + k, 4), 0, keepdims=False) for k in range(4)]
    return [taken[0]] + [moved(taken[k], TM, k) for k in range(1, 4)]


def local(
    tokens, region_ids, first_gain, first_bias, input_weight, input_bias, output_weight, output_bias,
    second_gain, second_bias, expand_weight, expand_bias, reduce_weight, reduce_bias, merge_gain, merge_bias,
    merge_weight, cotangent,
):
    merged_count = cotangent.shape[0] * cotangent.shape[1] * cotangent.shape[2] * lax.axis_size("height")
    factor = 1.0 / math.sqrt(merged_count)

    from_tm = moved(tokens[:4, 3:], TM, -1)
    from_rows = moved(tokens[4:, :3], ROWS, -1)
    from_both = moved(tokens[:4, :3], BOTH, -1)
    field = jnp.concatenate(
        [
            jnp.concatenate([tokens[4:, 3:], from_rows], 1),
            jnp.concatenate([from_tm, from_both], 1),
        ],
        0,
    )
    labels = region_ids.reshape(8, 2, 7, 2, 7).transpose(1, 3, 2, 4, 0).reshape(4, CELLS, 1)
    cot = lax.all_to_all(split_frames(cotangent), "tm", 0, 0, tiled=True)

    attn = (first_gain, first_bias, input_weight, input_bias, output_weight, output_bias)
    res1, x1, qkv1, ctx1, eq1 = attend(1, field, labels, *attn)
    above = moved(res1[:, 224:], ROWS, 1)
    res0, x0, qkv0, ctx0, eq0 = attend(0, field, labels, *attn)
    params = (
        second_gain, second_bias, expand_weight, expand_bias, reduce_weight, reduce_bias, merge_gain, merge_bias,
        merge_weight,
    )
    merged_first, dabove, d0_first, *kept, vec_first = post_first(above, res0, cot, params)
    below = moved(dabove, ROWS, -1)
    merged_parts, d0, d1, early, vec_post = post_second(
        res0, res1, cot, params, vec_first, merged_first, d0_first, kept
    )
    below, early = lax.optimization_barrier((below, early))
    early_parts = exchange(early.reshape(128, EARLY, 128))
    merged_pieces = rotate_frames(merged_parts, 1)

    back = (first_gain, first_bias, input_weight, output_weight)
    g0, *sums = attend_back(0, (d0,), (x0, qkv0, ctx0, eq0), labels, back, ())
    g1, late = attend_back(1, (d1, below), (x1, qkv1, ctx1, eq1), labels, back, sums + [vec_post])
    early_parts, merged_pieces = lax.optimization_barrier((early_parts, merged_pieces))
    second = exchange(sum_early(factor, early_parts, late))

    pieces = (
        moved(g0[4:], TM, 1),
        moved(g1[4:, :4], TM, 1),
        moved(g1[:4, 4:], ROWS, 1),
        moved(g1[4:, 4:], BOTH, 1),
    )

    second, pieces = lax.optimization_barrier((second, pieces))
    others = lax.ppermute(second[:, :HALF], "tm", [(0, 1), (1, 0), (2, 3), (3, 2)])
    (third,) = on_device(
        functools.partial(sum_late_kernel, factor), [((128, LATE, 128), BF16)], (second,), [], 24, 10**6
    )
    third = exchange(third)
    merged = join_frames(*merged_pieces)
    to_tm0, to_tm1, to_rows, to_both = pieces
    grad_tokens = jnp.concatenate(
        [
            jnp.concatenate([to_both, to_tm0, to_tm1], 1),
            jnp.concatenate([to_rows, g0[:4], g1[:4, :4]], 1),
        ],
        0,
    )
    dwe, dwr, dwm = unpack(unpack_early_kernel, (second, others), [(256, 1024), (1024, 256), (1024, 512)])
    third, dwe, dwr, dwm, merged, grad_tokens = lax.optimization_barrier(
        (third, dwe, dwr, dwm, merged, grad_tokens)
    )
    lengths = [(128 * count,) for _, _, count in VECTORS]
    dwi, dwo, *vecs = unpack(unpack_late_kernel, (third,), [(256, 768), (256, 256)] + lengths)
    return (
        merged, grad_tokens, vecs[0], vecs[1], dwi, vecs[2], dwo, vecs[3], vecs[4], vecs[5], dwe, vecs[6], dwr,
        vecs[7], vecs[8], vecs[9], dwm,
    )


def solution(mesh):
    in_specs = (
        (P("tm", "height", None, None), P("tm", "height", None))
        + (P(),) * 15
        + (P(None, "height", None, "tm"),)
    )
    out_specs = (P(None, "height", None, "tm"), P("tm", "height", None, None)) + (P(),) * 15
    return jax.shard_map(local, mesh=mesh, in_specs=in_specs, out_specs=out_specs, check_vma=False)
```

time: 235 us -> 196 us (0.83)
  blocking collectives: 43.7 us -> 0 us
  local copies, waits for them, and re-layouts: 41.3 us -> 15 us
  Pallas kernels: 64.9 us -> 91 us
  starting transfers between devices: 37.4 us -> 49.2 us
  waiting for transfers between devices: 40 us -> 36.6 us
  other arithmetic: 5.49 us -> 2.16 us
    all_to_all x1 -> x0, blocking collectives: 43.7 us -> none  [spread_sum(): parts = lax.all_to_all(slabs.reshape(128, n, 128), BOTH, 0, 0, tiled=True)]
    pallas_call x7 -> x12, Pallas kernels: 64.9 us -> 91 us  [on_device(): pl.pallas_call(kernel, grid=(steps,), in_specs=specs([a.shape for a in in...]
    unnamed x83 -> x45, local copies, waits for them, and re-layouts: 26.6 us -> 9.04 us
    all_to_all x2 -> x3, starting transfers between devices: 10.1 us -> 18.8 us  [exchange(): return lax.all_to_all(parts, BOTH, 0, 0, tiled=True)]
    ppermute x8 -> x12, waiting for transfers between devices: 34.1 us -> 27.7 us  [moved(): return lax.ppermute(value, axis if len(axis) > 1 else axis[0], pairs)]
    transpose x5 -> x0, local copies, waits for them, and re-layouts: 4.11 us -> none  [unslab(): return part.transpose(1, 0, 2).reshape(rows, count * 128)]
    ppermute x8 -> x12, starting transfers between devices: 22.5 us -> 26.1 us  [moved(): return lax.ppermute(value, axis if len(axis) > 1 else axis[0], pairs)]
    all_to_all x2 -> x3, waiting for transfers between devices: 5.89 us -> 8.87 us  [exchange(): return lax.all_to_all(parts, BOTH, 0, 0, tiled=True)]
  transfers between devices with their start and end apart: 11 -> 17, of which waited for: 2 -> 4; matrix products, arithmetic and copies ran while one was open for 7% -> 4% of each run, Pallas kernels for 11% -> 38%
where the time goes in v2:
time: 196 us; the launch traced here: 195 us
  Pallas kernels  91 us (46%)
  starting transfers between devices  49.2 us (25%)
  waiting for transfers between devices  36.6 us (19%)
  local copies, waits for them, and re-layouts  15 us (8%)
  other arithmetic  2.16 us (1%)
    pallas_call x12, Pallas kernels, on_device(): pl.pallas_call(kernel, grid=(steps,), in_specs=specs([a.shape for a in in...  91 us
    ppermute x12, waiting for transfers between devices, moved(): return lax.ppermute(value, axis if len(axis) > 1 else axis[0], pairs)  27.7 us
    ppermute x12, starting transfers between devices, moved(): return lax.ppermute(value, axis if len(axis) > 1 else axis[0], pairs)  26.1 us
    all_to_all x3, starting transfers between devices, exchange(): return lax.all_to_all(parts, BOTH, 0, 0, tiled=True)  18.8 us
    unnamed x45, local copies, waits for them, and re-layouts  9.04 us
    all_to_all x3, waiting for transfers between devices, exchange(): return lax.all_to_all(parts, BOTH, 0, 0, tiled=True)  8.87 us
    all_to_all x1, starting transfers between devices, local(): cot = lax.all_to_all(split_frames(cotangent), 'tm', 0, 0, tiled=True)  4.21 us
  transfers between devices with their start and end apart: 17, of which 4 were waited for; matrix products, arithmetic and copies ran while one was open for 4% of the time, Pallas kernels for 38%

profile of v2, /device:TPU:1, one launch (start us, length us, event | category | flops | bytes accessed | tf_op | source)
XLA Modules:
  0.0 195.1 jit_solution(265020818234534721)
XLA Ops:
  4.9 8.7 %collective-permute-start.2 = (bf16[4,3,14,256]{3,2,1,0:T(8,128)(2,1)S(1)}, bf16[4,3,14,256]{3,2,1,0:T(8,128)(2,1)S(1)}, u32[]{:S(2)}, u32[]{:S(2)}) collective-permute-start(bf16[4,3,14,256]{3,2,1,0:T(8,128)(2,1)S(1)} %copy.58), channel_id=1, source_target_pairs={{0,127},{1,96},{2,97},{3,98},{4,99},{5,100},{6,101},{7,102},{8,103... | collective-permute-start | bytes 258056 | tf_op jit(solution)/shard_map/ppermute | solution.py:508
  14.8 2.0 %shard_map.307 = bf16[4,7,56,128]{3,2,1,0:T(8,128)(2,1)} custom-call(bf16[32,7,7,128]{3,2,1,0:T(8,128)(2,1)} %copy.50.cot_ref), custom_call_target="tpu_custom_call" | custom-call | flops 1000000 | bytes 4000000 | tf_op jit(solution)/shard_map/pallas_call | solution.py:147
  16.7 4.2 %all-to-all-start = ((bf16[4,7,56,128]{3,2,1,0:T(8,128)(2,1)}), bf16[4,7,56,128]{3,2,1,0:T(8,128)(2,1)S(1)}, u32[]{:S(2)}, u32[]{:S(2)}) async-start(bf16[4,7,56,128]{3,2,1,0:T(8,128)(2,1)} %shard_map.307), calls=%async_computation | async-start | bytes 802816 | tf_op jit(solution)/shard_map/all_to_all | solution.py:618
  23.6 7.8 %shard_map.305 = (bf16[2,392,256]{2,1,0:T(8,128)(2,1)}, bf16[2,392,256]{2,1,0:T(8,128)(2,1)}, bf16[2,392,768]{2,1,0:T(8,128)(2,1)}, bf16[2,392,256]{2,1,0:T(8,128)(2,1)}, bf16[2,392,128]{2,1,0:T(8,128)(2,1)}) custom-call(bf16[8,14,14,256]{3,2,1,0:T(8,128)(2,1)} %maximum_maximum_fusion.tok_ref, s32[4,392,1]{2,1,0:T(8,128)} %reshape.46.lab_ref.refs_5_.refs_6_, ...), custom_call_target="tpu_custom_call" | custom-call | flops 4000000000 | bytes 4000000 | tf_op jit(solution)/shard_map/pallas_call | solution.py:147
  33.4 7.8 %shard_map.306 = (bf16[2,392,256]{2,1,0:T(8,128)(2,1)}, bf16[2,392,256]{2,1,0:T(8,128)(2,1)}, bf16[2,392,768]{2,1,0:T(8,128)(2,1)}, bf16[2,392,256]{2,1,0:T(8,128)(2,1)}, bf16[2,392,128]{2,1,0:T(8,128)(2,1)}) custom-call(bf16[8,14,14,256]{3,2,1,0:T(8,128)(2,1)} %maximum_maximum_fusion.tok_ref, s32[4,392,1]{2,1,0:T(8,128)} %reshape.46.lab_ref.refs_5_.refs_6_, ...), custom_call_target="tpu_custom_call" | custom-call | flops 4000000000 | bytes 4000000 | tf_op jit(solution)/shard_map/pallas_call | solution.py:147
  43.2 9.1 %shard_map.308 = (bf16[4,2,56,128]{3,2,1,0:T(8,128)(2,1)}, bf16[2,168,256]{2,1,0:T(8,128)(2,1)}, f32[2,56,256]{2,1,0:T(8,128)}, bf16[448,256]{1,0:T(8,128)(2,1)}...) custom-call(bf16[2,168,256]{2,1,0:T(8,128)(2,1)} %copy-done.18, ...), custom_call_target="tpu_custom_call" | custom-call | flops 4000000000 | bytes 4000000 | tf_op jit(solution)/shard_map/pallas_call | solution.py:147
  52.3 3.7 %collective-permute-start.4 = (bf16[2,168,256]{2,1,0:T(8,128)(2,1)}, bf16[2,168,256]{2,1,0:T(8,128)(2,1)S(1)}, u32[]{:S(2)}, u32[]{:S(2)}) collective-permute-start(bf16[2,168,256]{2,1,0:T(8,128)(2,1)} %get-tuple-element.83), channel_id=1, source_target_pairs={{0,31},{1,0},{2,1},{3,2},{4,3},{5,4},{6,5},{7,6},{8,7},{9,8},{10,9... | collective-permute-start | bytes 516104 | tf_op jit(solution)/shard_map/ppermute | solution.py:508
  56.0 20.2 %shard_map.309 = (bf16[4,7,56,128]{3,2,1,0:T(8,128)(2,1)}, bf16[2,392,256]{2,1,0:T(8,128)(2,1)}, bf16[2,224,256]{2,1,0:T(8,128)(2,1)}, bf16[8192,128]{1,0:T(8,128)(2,1)}, f32[8,1024]{1,0:T(8,128)}) custom-call(bf16[2,392,256]{2,1,0:T(8,128)(2,1)} %get-tuple-element.82.res0_ref, bf16[2,392,256]{2,1,0:T(8,128)(2,1)} %get-tuple-element.81.res1_ref, ...), custom_call_target="tpu_custom_call" | custom-call | flops 11000000512 | bytes 4000000 | tf_op jit(solution)/shard_map/pallas_call | solution.py:147
  76.9 5.0 %all-to-all-start.1 = ((bf16[128,64,128]{2,1,0:T(8,128)(2,1)}), bf16[128,64,128]{2,1,0:T(8,128)(2,1)S(1)}, u32[]{:S(2)}, u32[]{:S(2)}) async-start(bf16[128,64,128]{2,1,0:T(8,128)(2,1)} %bitcast.12), calls=%async_computation.1 | async-start | bytes 4194304 | tf_op jit(solution)/shard_map/all_to_all | solution.py:553
  82.6 3.1 %collective-permute-start.5 = (bf16[7,56,128]{2,1,0:T(8,128)(2,1)S(1)}, bf16[7,56,128]{2,1,0:T(8,128)(2,1)S(1)}, u32[]{:S(2)}, u32[]{:S(2)}) collective-permute-start(bf16[7,56,128]{2,1,0:T(8,128)(2,1)S(1)} %get-tuple-element.191), channel_id=1, source_target_pairs={{0,32},{32,64},{64,96},{96,0},{1,33},{33,65},{65,97},{97,1},{2,34}... | collective-permute-start | bytes 301064 | tf_op jit(solution)/shard_map/ppermute | solution.py:508
  86.5 14.1 %shard_map.310 = (bf16[8,7,14,256]{3,2,1,0:T(8,128)(2,1)}, f32[256,768]{1,0:T(8,128)}, f32[256,256]{1,0:T(8,128)}, f32[8,768]{1,0:T(8,128)}) custom-call(bf16[2,392,256]{2,1,0:T(8,128)(2,1)} %get-tuple-element.103.refs_0_, bf16[2,392,256]{2,1,0:T(8,128)(2,1)} %get-tuple-element.104.refs_1_, bf16[2,392,768]{2,1,0:T(8,128)(2,1)} %get-tuple-element.105.refs_2_, ...), custom_call_target="tpu_custom_call" | custom-call | flops 6000000000 | bytes 4000000 | tf_op jit(solution)/shard_map/pallas_call | solution.py:147
  100.6 14.6 %shard_map.311 = (bf16[8,7,14,256]{3,2,1,0:T(8,128)(2,1)}, bf16[128,24,128]{2,1,0:T(8,128)(2,1)}) custom-call(bf16[2,224,256]{2,1,0:T(8,128)(2,1)} %get-tuple-element.97.refs_0_, bf16[2,168,256]{2,1,0:T(8,128)(2,1)} %copy-done.17, bf16[2,392,256]{2,1,0:T(8,128)(2,1)} %get-tuple-element.99.refs_2_, bf16[2,392,768]{2,1,0:T(8,128)(2,1)} %get-tuple-element.100.refs_3_, ...), custom_call_target="tpu_custom_call" | custom-call | flops 6000000000 | bytes 4000000 | tf_op jit(solution)/shard_map/pallas_call | solution.py:147
  117.8 4.6 %shard_map.312 = bf16[128,56,128]{2,1,0:T(8,128)(2,1)} custom-call(bf16[128,64,128]{2,1,0:T(8,128)(2,1)} %copy-done.1, bf16[128,24,128]{2,1,0:T(8,128)(2,1)} %get-tuple-element.112.late_ref), custom_call_target="tpu_custom_call" | custom-call | flops 1000000 | bytes 4000000 | tf_op jit(solution)/shard_map/pallas_call | solution.py:147
  122.5 9.9 %all-to-all-start.2 = ((bf16[128,56,128]{2,1,0:T(8,128)(2,1)}), bf16[128,56,128]{2,1,0:T(8,128)(2,1)S(1)}, u32[]{:S(2)}, u32[]{:S(2)}) async-start(bf16[128,56,128]{2,1,0:T(8,128)(2,1)} %shard_map.312), calls=%async_computation.2 | async-start | bytes 3670016 | tf_op jit(solution)/shard_map/all_to_all | solution.py:553
  132.5 3.2 %collective-permute-start.8 = (bf16[4,7,14,256]{3,2,1,0:T(8,128)(2,1)S(1)}, bf16[4,7,14,256]{3,2,1,0:T(8,128)(2,1)S(1)}, u32[]{:S(2)}, u32[]{:S(2)}) collective-permute-start(bf16[4,7,14,256]{3,2,1,0:T(8,128)(2,1)S(1)} %get-tuple-element.184), channel_id=1, source_target_pairs={{0,32},{32,64},{64,96},{96,0},{1,33},{33,65},{65,97},{97,1},{2,34}... | collective-permute-start | bytes 602120 | tf_op jit(solution)/shard_map/ppermute | solution.py:508
  137.6 1.9 collective-permute-start.11
  139.5 14.9 %collective-permute-done.8 = bf16[4,7,14,256]{3,2,1,0:T(8,128)(2,1)S(1)} collective-permute-done((bf16[4,7,14,256]{3,2,1,0:T(8,128)(2,1)S(1)}, bf16[4,7,14,256]{3,2,1,0:T(8,128)(2,1)S(1)}, u32[]{:S(2)}, u32[]{:S(2)}) %collective-permute-start.8) | collective-permute-done | bytes 200736 | tf_op jit(solution)/shard_map/ppermute | solution.py:508
  154.4 11.5 %collective-permute-done.10 = bf16[4,3,14,256]{3,2,1,0:T(8,128)(2,1)S(1)} collective-permute-done((bf16[4,3,14,256]{3,2,1,0:T(8,128)(2,1)S(1)}, bf16[4,3,14,256]{3,2,1,0:T(8,128)(2,1)S(1)}, u32[]{:S(2)}, u32[]{:S(2)}) %collective-permute-start.10) | collective-permute-done | bytes 86048 | tf_op jit(solution)/shard_map/ppermute | solution.py:508
  167.8 2.6 %shard_map.313 = bf16[128,24,128]{2,1,0:T(8,128)(2,1)} custom-call(bf16[128,56,128]{2,1,0:T(8,128)(2,1)} %copy-done), custom_call_target="tpu_custom_call" | custom-call | flops 1000000 | bytes 4000000 | tf_op jit(solution)/shard_map/pallas_call | solution.py:147
  170.4 3.9 %all-to-all-start.3 = ((bf16[128,24,128]{2,1,0:T(8,128)(2,1)}), bf16[128,24,128]{2,1,0:T(8,128)(2,1)S(1)}, u32[]{:S(2)}, u32[]{:S(2)}) async-start(bf16[128,24,128]{2,1,0:T(8,128)(2,1)} %shard_map.313), calls=%async_computation.3 | async-start | bytes 1572864 | tf_op jit(solution)/shard_map/all_to_all | solution.py:553
  174.3 2.0 %shard_map.315 = bf16[32,7,7,128]{3,2,1,0:T(8,128)(2,1)} custom-call(bf16[7,56,128]{2,1,0:T(8,128)(2,1)} %get-tuple-element.119.p0_ref, bf16[7,56,128]{2,1,0:T(8,128)(2,1)} %copy-done.10, bf16[7,56,128]{2,1,0:T(8,128)(2,1)} %copy-done.11, bf16[7,56,128]{2,1,0:T(8,128)(2,1)} %collective-permute-done.7.p3_ref), custom_call_target="tpu_custom_call" | custom-call | flops 1000000 | bytes 4000000 | tf_op jit(solution)/shard_map/pallas_call | solution.py:147
  177.5 4.1 %shard_map.314 = (f32[256,1024]{1,0:T(8,128)}, f32[1024,256]{1,0:T(8,128)}, f32[1024,512]{1,0:T(8,128)}) custom-call(bf16[128,56,128]{2,1,0:T(8,128)(2,1)} %copy-done, bf16[128,32,128]{2,1,0:T(8,128)(2,1)} %collective-permute-done.12.other_ref), custom_call_target="tpu_custom_call" | custom-call | flops 1000000 | bytes 4000000 | tf_op jit(solution)/shard_map/pallas_call | solution.py:147
  181.6 8.9 %all-to-all-done.3.slab_ref = bf16[128,24,128]{2,1,0:T(8,128)(2,1)S(1)} async-done(((bf16[128,24,128]{2,1,0:T(8,128)(2,1)}), bf16[128,24,128]{2,1,0:T(8,128)(2,1)S(1)}, u32[]{:S(2)}, u32[]{:S(2)}) %all-to-all-start.3) | async-done | bytes 786464 | tf_op jit(solution)/shard_map/all_to_all | solution.py:553
  192.8 2.1 %shard_map.316 = (f32[256,768]{1,0:T(8,128)}, f32[256,256]{1,0:T(8,128)}, f32[256]{0:T(256)}, f32[256]{0:T(256)}, f32[768]{0:T(1024)}, /*index=5*/f32[256]{0:T(2...) custom-call(bf16[128,24,128]{2,1,0:T(8,128)(2,1)} %copy-done.2), custom_call_target="tpu_custom_call" | custom-call | flops 1000000 | bytes 4000000 | tf_op jit(solution)/shard_map/pallas_call | solution.py:147
  (80 shorter events, 24.0 us)
Async XLA Ops:
  0.7 13.2 %copy-start.8 = (bf16[32,7,7,128]{3,0,2,1:T(8,128)(2,1)S(1)}, bf16[32,7,7,128]{3,0,2,1:T(8,128)(2,1)}, u32[]{:S(2)}) copy-start(bf16[32,7,7,128]{3,0,2,1:T(8,128)(2,1)} %param.35) | copy-start | bytes 1204228
  2.3 20.3 %collective-permute-start.1 = (bf16[4,11,14,256]{3,2,1,0:T(8,128)(2,1)S(1)}, bf16[4,11,14,256]{3,2,1,0:T(8,128)(2,1)S(1)}, u32[]{:S(2)}, u32[]{:S(2)}) collective-permute-start(bf16[4,11,14,256]{3,2,1,0:T(8,128)(2,1)S(1)} %copy.57), channel_id=1, source_target_pairs={{0,96},{32,0},{64,32},{96,64},{1,97},{33,1},{65,33},{97,65},{2,98}... | collective-permute-start | bytes 946184 | tf_op jit(solution)/shard_map/ppermute | solution.py:508
  4.9 16.1 %copy-start.16 = (s32[8,14,14]{2,0,1:T(8,128)S(1)}, s32[8,14,14]{2,0,1:T(8,128)}, u32[]{:S(2)}) copy-start(s32[8,14,14]{2,0,1:T(8,128)} %param.19) | copy-start | bytes 18820
  4.9 17.7 %collective-permute-start.2 = (bf16[4,3,14,256]{3,2,1,0:T(8,128)(2,1)S(1)}, bf16[4,3,14,256]{3,2,1,0:T(8,128)(2,1)S(1)}, u32[]{:S(2)}, u32[]{:S(2)}) collective-permute-start(bf16[4,3,14,256]{3,2,1,0:T(8,128)(2,1)S(1)} %copy.58), channel_id=1, source_target_pairs={{0,127},{1,96},{2,97},{3,98},{4,99},{5,100},{6,101},{7,102},{8,103... | collective-permute-start | bytes 258056 | tf_op jit(solution)/shard_map/ppermute | solution.py:508
  13.6 8.9 %collective-permute-start = (bf16[4,3,14,256]{3,2,1,0:T(8,128)(2,1)S(1)}, bf16[4,3,14,256]{3,2,1,0:T(8,128)(2,1)S(1)}, u32[]{:S(2)}, u32[]{:S(2)}) collective-permute-start(bf16[4,3,14,256]{3,2,1,0:T(8,128)(2,1)S(1)} %copy.56), channel_id=1, source_target_pairs={{0,31},{1,0},{2,1},{3,2},{4,3},{5,4},{6,5},{7,6},{8,7},{9,8},{10,9... | collective-permute-start | bytes 258056 | tf_op jit(solution)/shard_map/ppermute | solution.py:508
  16.7 24.5 %all-to-all-start = ((bf16[4,7,56,128]{3,2,1,0:T(8,128)(2,1)}), bf16[4,7,56,128]{3,2,1,0:T(8,128)(2,1)S(1)}, u32[]{:S(2)}, u32[]{:S(2)}) async-start(bf16[4,7,56,128]{3,2,1,0:T(8,128)(2,1)} %shard_map.307), calls=%async_computation | async-start | bytes 802816 | tf_op jit(solution)/shard_map/all_to_all | solution.py:618
  32.3 10.2 %collective-permute-start.3 = (bf16[2,168,256]{2,1,0:T(8,128)(2,1)S(1)}, bf16[2,168,256]{2,1,0:T(8,128)(2,1)S(1)}, u32[]{:S(2)}, u32[]{:S(2)}) collective-permute-start(bf16[2,168,256]{2,1,0:T(8,128)(2,1)S(1)} %slice.40), channel_id=1, source_target_pairs={{0,1},{1,2},{2,3},{3,4},{4,5},{5,6},{6,7},{7,8},{8,9},{9,10},{10,1... | collective-permute-start | bytes 516104 | tf_op jit(solution)/shard_map/ppermute | solution.py:508
  52.3 23.9 %collective-permute-start.4 = (bf16[2,168,256]{2,1,0:T(8,128)(2,1)}, bf16[2,168,256]{2,1,0:T(8,128)(2,1)S(1)}, u32[]{:S(2)}, u32[]{:S(2)}) collective-permute-start(bf16[2,168,256]{2,1,0:T(8,128)(2,1)} %get-tuple-element.83), channel_id=1, source_target_pairs={{0,31},{1,0},{2,1},{3,2},{4,3},{5,4},{6,5},{7,6},{8,7},{9,8},{10,9... | collective-permute-start | bytes 516104 | tf_op jit(solution)/shard_map/ppermute | solution.py:508
  76.9 39.6 %all-to-all-start.1 = ((bf16[128,64,128]{2,1,0:T(8,128)(2,1)}), bf16[128,64,128]{2,1,0:T(8,128)(2,1)S(1)}, u32[]{:S(2)}, u32[]{:S(2)}) async-start(bf16[128,64,128]{2,1,0:T(8,128)(2,1)} %bitcast.12), calls=%async_computation.1 | async-start | bytes 4194304 | tf_op jit(solution)/shard_map/all_to_all | solution.py:553
  82.6 32.6 %collective-permute-start.5 = (bf16[7,56,128]{2,1,0:T(8,128)(2,1)S(1)}, bf16[7,56,128]{2,1,0:T(8,128)(2,1)S(1)}, u32[]{:S(2)}, u32[]{:S(2)}) collective-permute-start(bf16[7,56,128]{2,1,0:T(8,128)(2,1)S(1)} %get-tuple-element.191), channel_id=1, source_target_pairs={{0,32},{32,64},{64,96},{96,0},{1,33},{33,65},{65,97},{97,1},{2,34}... | collective-permute-start | bytes 301064 | tf_op jit(solution)/shard_map/ppermute | solution.py:508
  85.7 29.5 %collective-permute-start.6 = (bf16[7,56,128]{2,1,0:T(8,128)(2,1)S(1)}, bf16[7,56,128]{2,1,0:T(8,128)(2,1)S(1)}, u32[]{:S(2)}, u32[]{:S(2)}) collective-permute-start(bf16[7,56,128]{2,1,0:T(8,128)(2,1)S(1)} %get-tuple-element.190), channel_id=1, source_target_pairs={{0,64},{32,96},{64,0},{96,32},{1,65},{33,97},{65,1},{97,33},{2,66}... | collective-permute-start | bytes 301064 | tf_op jit(solution)/shard_map/ppermute | solution.py:508
  86.5 30.0 %collective-permute-start.7 = (bf16[7,56,128]{2,1,0:T(8,128)(2,1)S(1)}, bf16[7,56,128]{2,1,0:T(8,128)(2,1)}, u32[]{:S(2)}, u32[]{:S(2)}) collective-permute-start(bf16[7,56,128]{2,1,0:T(8,128)(2,1)S(1)} %get-tuple-element.189), channel_id=1, source_target_pairs={{0,96},{32,0},{64,32},{96,64},{1,97},{33,1},{65,33},{97,65},{2,98}... | collective-permute-start | bytes 301064 | tf_op jit(solution)/shard_map/ppermute | solution.py:508
  122.5 10.0 %copy-start.4 = (bf16[8,7,14,256]{3,2,1,0:T(8,128)(2,1)S(1)}, bf16[8,7,14,256]{3,2,1,0:T(8,128)(2,1)}, u32[]{:S(2)}) copy-start(bf16[8,7,14,256]{3,2,1,0:T(8,128)(2,1)} %get-tuple-element.113) | copy-start | bytes 1204228
  122.5 13.2 %copy-start.5 = (bf16[8,7,14,256]{3,2,1,0:T(8,128)(2,1)S(1)}, bf16[8,7,14,256]{3,2,1,0:T(8,128)(2,1)}, u32[]{:S(2)}) copy-start(bf16[8,7,14,256]{3,2,1,0:T(8,128)(2,1)} %get-tuple-element.114) | copy-start | bytes 1204228
  122.5 44.1 %all-to-all-start.2 = ((bf16[128,56,128]{2,1,0:T(8,128)(2,1)}), bf16[128,56,128]{2,1,0:T(8,128)(2,1)S(1)}, u32[]{:S(2)}, u32[]{:S(2)}) async-start(bf16[128,56,128]{2,1,0:T(8,128)(2,1)} %shard_map.312), calls=%async_computation.2 | async-start | bytes 3670016 | tf_op jit(solution)/shard_map/all_to_all | solution.py:553
  132.5 21.9 %collective-permute-start.8 = (bf16[4,7,14,256]{3,2,1,0:T(8,128)(2,1)S(1)}, bf16[4,7,14,256]{3,2,1,0:T(8,128)(2,1)S(1)}, u32[]{:S(2)}, u32[]{:S(2)}) collective-permute-start(bf16[4,7,14,256]{3,2,1,0:T(8,128)(2,1)S(1)} %get-tuple-element.184), channel_id=1, source_target_pairs={{0,32},{32,64},{64,96},{96,0},{1,33},{33,65},{65,97},{97,1},{2,34}... | collective-permute-start | bytes 602120 | tf_op jit(solution)/shard_map/ppermute | solution.py:508
  135.7 30.2 %collective-permute-start.9 = (bf16[4,4,14,256]{3,2,1,0:T(8,128)(2,1)S(1)}, bf16[4,4,14,256]{3,2,1,0:T(8,128)(2,1)S(1)}, u32[]{:S(2)}, u32[]{:S(2)}) collective-permute-start(bf16[4,4,14,256]{3,2,1,0:T(8,128)(2,1)S(1)} %get-tuple-element.186), channel_id=1, source_target_pairs={{0,32},{32,64},{64,96},{96,0},{1,33},{33,65},{65,97},{97,1},{2,34}... | collective-permute-start | bytes 344072 | tf_op jit(solution)/shard_map/ppermute | solution.py:508
  136.2 29.7 %collective-permute-start.10 = (bf16[4,3,14,256]{3,2,1,0:T(8,128)(2,1)S(1)}, bf16[4,3,14,256]{3,2,1,0:T(8,128)(2,1)S(1)}, u32[]{:S(2)}, u32[]{:S(2)}) collective-permute-start(bf16[4,3,14,256]{3,2,1,0:T(8,128)(2,1)S(1)} %get-tuple-element.188), channel_id=1, source_target_pairs={{0,1},{1,2},{2,3},{3,4},{4,5},{5,6},{6,7},{7,8},{8,9},{9,10},{10,1... | collective-permute-start | bytes 258056 | tf_op jit(solution)/shard_map/ppermute | solution.py:508
  137.6 28.3 %collective-permute-start.11 = (bf16[4,3,14,256]{3,2,1,0:T(8,128)(2,1)S(1)}, bf16[4,3,14,256]{3,2,1,0:T(8,128)(2,1)S(1)}, u32[]{:S(2)}, u32[]{:S(2)}) collective-permute-start(bf16[4,3,14,256]{3,2,1,0:T(8,128)(2,1)S(1)} %get-tuple-element.187), channel_id=1, source_target_pairs={{0,33},{1,34},{2,35},{3,36},{4,37},{5,38},{6,39},{7,40},{8,41},{9,... | collective-permute-start | bytes 258056 | tf_op jit(solution)/shard_map/ppermute | solution.py:508
  154.4 11.5 %copy-start.9 = (bf16[4,7,14,256]{3,2,1,0:T(8,128)(2,1)}, bf16[4,7,14,256]{3,2,1,0:T(8,128)(2,1)S(1)}, u32[]{:S(2)}) copy-start(bf16[4,7,14,256]{3,2,1,0:T(8,128)(2,1)S(1)} %collective-permute-done.8) | copy-start | bytes 602116
  166.6 10.9 %collective-permute-start.12 = (bf16[128,32,128]{2,1,0:T(8,128)(2,1)S(1)}, bf16[128,32,128]{2,1,0:T(8,128)(2,1)}, u32[]{:S(2)}, u32[]{:S(2)}) collective-permute-start(bf16[128,32,128]{2,1,0:T(8,128)(2,1)S(1)} %slice.45), channel_id=1, source_target_pairs={{0,32},{32,0},{64,96},{96,64},{1,33},{33,1},{65,97},{97,65},{2,34}... | collective-permute-start | bytes 3145736 | tf_op jit(solution)/shard_map/ppermute | solution.py:651
  170.4 6.0 %copy-start.15 = (bf16[4,3,14,256]{3,2,1,0:T(8,128)(2,1)S(1)}, bf16[4,3,14,256]{3,2,1,0:T(8,128)(2,1)}, u32[]{:S(2)}) copy-start(bf16[4,3,14,256]{3,2,1,0:T(8,128)(2,1)} %copy-done.14) | copy-start | bytes 258052
  170.4 20.1 %all-to-all-start.3 = ((bf16[128,24,128]{2,1,0:T(8,128)(2,1)}), bf16[128,24,128]{2,1,0:T(8,128)(2,1)S(1)}, u32[]{:S(2)}, u32[]{:S(2)}) async-start(bf16[128,24,128]{2,1,0:T(8,128)(2,1)} %shard_map.313), calls=%async_computation.3 | async-start | bytes 1572864 | tf_op jit(solution)/shard_map/all_to_all | solution.py:553
  177.5 13.0 %copy-start.3 = (bf16[32,7,7,128]{3,2,1,0:T(8,128)(2,1)S(1)}, bf16[32,7,7,128]{3,2,1,0:T(8,128)(2,1)}, u32[]{:S(2)}) copy-start(bf16[32,7,7,128]{3,2,1,0:T(8,128)(2,1)} %shard_map.315) | copy-start | bytes 1204228
  (12 other events, 21.8 us)
